TPU v7x, 512 devices: a whole 4x4x16 slice. The times are simulated.
512 devices in a mesh: ctx: 128 (over y_lo, z, x), ch: 4 (over y_hi, core).
Axes of the slice: x: 4, y: 4 (y_hi: 2, y_lo: 2; y = y_hi * 2 + y_lo), z: 16, core: 2. Of those that a mesh axis runs over, the one named last changes fastest.
Arguments:
- q_branch: bfloat16 [4096, 16384], P('ch', 'ctx'), may hold values from -6 to 6
- k_branch: bfloat16 [4096, 16384], P('ch', 'ctx'), may hold values from -6 to 6
- v_branch: bfloat16 [4096, 16384], P('ch', 'ctx'), may hold values from -6 to 6
- grad_gated: bfloat16 [4096, 16384], P('ch', 'ctx'), may hold values from -6 to 6
- decay_rates: float32 [256, 16], replicated, as said below
- residue: float32 [256, 16], replicated, may hold values from -1.5 to 1.5
Outputs:
- grad_q: bfloat16 [4096, 16384], P('ch', 'ctx')
- grad_k: bfloat16 [4096, 16384], P('ch', 'ctx')
- grad_v: bfloat16 [4096, 16384], P('ch', 'ctx')
- grad_residue: float32 [256, 16], replicated
Inputs may be any that keep to these rules, and one draw needn't show every extreme that they name: `decay_rates`: every rate lies between 0.05 / 16384 and 1 / 30.
All inputs are finite; a program needn't handle non-finite values.
Results may differ from a plain program's by a relative error of at most 0.0029.
Values sent between devices are 32-bit elements; how exact they have to be, the bound alone decides.
A program may use at most 128 MiB of HBM per device.

v0:
```python
import math

import jax
import jax.numpy as jnp
from jax import lax
from jax.sharding import PartitionSpec as P

FGROUPS = 256
MODES = 16


def entering(value, axis, join, neutral, backward):
    count, mine = (lax.axis_size(axis), lax.axis_index(axis))
    pieces = jax.tree.map(lambda part: lax.all_gather(part, axis), value)
    if backward:
        pieces = jax.tree.map(lambda part: part[::-1], pieces)
        mine = count - 1 - mine
    running = jax.tree.map(
        lambda part, zero: jnp.full_like(part, 0) + jnp.asarray(zero, part.dtype), value, neutral
    )

    def hop(position, running):
        longer = join(running, jax.tree.map(lambda part: part[position], pieces))
        return jax.tree.map(lambda new, old: jnp.where(position < mine, new, old), longer, running)

    return lax.fori_loop(0, count - 1, hop, running)


def combine(earlier, later):
    return (earlier[0] * later[0], later[0] * earlier[1] + later[1])


def carries(block_decay, forward_end, adjoint_start):
    identity = (jnp.ones_like(block_decay), jnp.zeros_like(forward_end))
    forward_in = entering((block_decay, forward_end), "ctx", combine, identity, False)[1]
    adjoint_in = entering((block_decay, adjoint_start), "ctx", combine, identity, True)[1]
    return (forward_in, adjoint_in)


def prefix_pair(product_kv, gated_grad, rate_col, positions, upper, lower):
    growth = jnp.exp(rate_col * positions[None, :])
    shrink = jnp.exp(-rate_col * positions[None, :])
    lifted = product_kv * growth
    lowered = gated_grad * shrink
    forward_part = jnp.dot(
        lifted, upper, precision=lax.Precision.HIGHEST, preferred_element_type=jnp.float32
    )
    adjoint_part = jnp.dot(
        lowered, lower, precision=lax.Precision.HIGHEST, preferred_element_type=jnp.float32
    )
    return (growth, shrink, lowered, forward_part, adjoint_part)


def local(q_branch, k_branch, v_branch, grad_gated, decay_rates, residue):
    channels = q_branch.shape[0]
    rows_here = q_branch.shape[1]
    total_rows = rows_here * lax.axis_size("ctx")
    norm_factor = 1.0 / math.sqrt(total_rows)
    repeats = channels // FGROUPS
    rates = jnp.tile(decay_rates, (repeats, 1))
    scaled = jnp.tile(residue, (repeats, 1)) * jnp.sqrt(2.0 * rates)
    query_float = q_branch.astype(jnp.float32)
    key_float = k_branch.astype(jnp.float32)
    value_float = v_branch.astype(jnp.float32)
    product_kv = key_float * value_float
    cotangent = grad_gated.astype(jnp.float32)
    gated_grad = cotangent * query_float
    positions = jnp.arange(rows_here, dtype=jnp.float32)
    row_ids = jnp.arange(rows_here, dtype=jnp.int32)
    upper = (row_ids[:, None] <= row_ids[None, :]).astype(jnp.float32)
    lower = (row_ids[:, None] >= row_ids[None, :]).astype(jnp.float32)
    block_decay = jnp.exp(-rates * rows_here)
    step_decay = jnp.exp(-rates)
    conv_out = jnp.zeros(q_branch.shape, jnp.float32)
    conv_grad = jnp.zeros(q_branch.shape, jnp.float32)
    res_cols = []
    end_cols = []
    start_cols = []
    for mode_index in range(MODES):
        rate_col = rates[:, mode_index, None]
        weight_col = scaled[:, mode_index, None]
        growth, shrink, lowered, forward_part, adjoint_part = prefix_pair(
            product_kv, gated_grad, rate_col, positions, upper, lower
        )
        conv_out = conv_out + weight_col * shrink * forward_part
        conv_grad = conv_grad + weight_col * growth * adjoint_part
        res_cols.append(jnp.sum(lowered * forward_part, axis=1))
        end_cols.append(forward_part[:, -1] * jnp.exp(-rates[:, mode_index] * (rows_here - 1.0)))
        start_cols.append(adjoint_part[:, 0])
    forward_end = jnp.stack(end_cols, axis=1)
    adjoint_start = jnp.stack(start_cols, axis=1)
    forward_in, adjoint_in = carries(block_decay, forward_end, adjoint_start)
    for mode_index in range(MODES):
        rate_col = rates[:, mode_index, None]
        rise = jnp.exp(-rate_col * (positions[None, :] + 1.0))
        fall = jnp.exp(-rate_col * (rows_here - positions[None, :]))
        conv_out = conv_out + scaled[:, mode_index, None] * rise * forward_in[:, mode_index, None]
        conv_grad = conv_grad + scaled[:, mode_index, None] * fall * adjoint_in[:, mode_index, None]
    res_sums = jnp.stack(res_cols, axis=1) + step_decay * adjoint_start * forward_in
    grad_q = (cotangent * conv_out).astype(jnp.bfloat16)
    grad_k = (conv_grad * value_float).astype(jnp.bfloat16)
    grad_v = (conv_grad * key_float).astype(jnp.bfloat16)
    per_channel = jnp.sqrt(2.0 * rates) * res_sums * norm_factor
    grouped = jnp.sum(per_channel.reshape(repeats, FGROUPS, MODES), axis=0)
    grad_residue = lax.psum(grouped, ("ctx", "ch"))
    return (grad_q, grad_k, grad_v, grad_residue)


def solution(mesh):
    in_specs = (P("ch", "ctx"), P("ch", "ctx"), P("ch", "ctx"), P("ch", "ctx"), P(), P())
    out_specs = (P("ch", "ctx"), P("ch", "ctx"), P("ch", "ctx"), P())
    return jax.shard_map(local, mesh=mesh, in_specs=in_specs, out_specs=out_specs, check_vma=False)
```

profile of v0, /device:TPU:1, one launch (start us, length us, event | category | flops | bytes accessed | tf_op | source)
XLA Modules:
  0.0 2085.5 jit_solution(16449494093350742199)
XLA Ops:
  21.9 2.2 multiply_reduce_fusion.1
  24.9 1.3 stack.73
  46.4 1.2 fusion.82
  49.9 1.3 stack.74
  51.8 2.5 multiply_reduce_fusion
  55.0 496.3 %all-gather.8.cloned.1.call-done = f32[131072,16]{0,1:T(8,128)} async-done(((f32[1024,16]{0,1:T(8,128)}), f32[131072,16]{0,1:T(8,128)}) %all-gather.8.cloned.1.call-update) | async-done | bytes 8388624 | tf_op jit(solution)/shard_map/all_gather | solution.py:14
  551.3 11.7 copy.32
  563.0 583.5 %all-gather.6.cloned.1.call-done = f32[128,1024,16]{1,2,0:T(8,128)} async-done(((f32[1,1024,16]{1,2,0:T(8,128)}), f32[128,1024,16]{1,2,0:T(8,128)}) %all-gather.6.cloned.1.call-update) | async-done | bytes 8388624 | tf_op jit(solution)/shard_map/all_gather | solution.py:14
  1146.5 256.1 %while.28 = (s32[]{:T(128)}, f32[1024,16]{0,1:T(8,128)S(1)}, s32[]{:T(128)}, f32[128,1024,16]{1,2,0:T(8,128)}, f32[128,1024,16]{1,0,2:T(8,128)}, /*index=5*/s32[]{:T(128)}, s32[]{:T(128)}) while((s32[]{:T(128)}, f32[1024,16]{0,1:T(8,128)S(1)}, s32[]{:T(128)}, f32[128,1024,16]{1,2,0:T(8,128)}, f32[128,1024,16]{1,0,2:T(8,128)}, ...), condition=%wide.region_1.0_spmd.clone, body=%wide.region_0.0_spmd.clone.sunk | while | flops 65540 | bytes 393329 | solution.py:26
  1148.5 1.1 constant_dynamic-slice_fusion.2
  1150.5 1.1 constant_dynamic-slice_fusion.2
  1152.5 1.1 constant_dynamic-slice_fusion.2
  1154.5 1.1 constant_dynamic-slice_fusion.2
  1158.6 1.1 constant_dynamic-slice_fusion.2
  1160.6 1.1 constant_dynamic-slice_fusion.2
  1162.6 1.1 constant_dynamic-slice_fusion.2
  1166.6 1.1 constant_dynamic-slice_fusion.2
  1168.7 1.1 constant_dynamic-slice_fusion.2
  1170.7 1.1 constant_dynamic-slice_fusion.2
  1172.7 1.1 constant_dynamic-slice_fusion.2
  1176.7 1.1 constant_dynamic-slice_fusion.2
  1178.7 1.1 constant_dynamic-slice_fusion.2
  1180.8 1.1 constant_dynamic-slice_fusion.2
  1182.8 1.1 constant_dynamic-slice_fusion.2
  1186.8 1.1 constant_dynamic-slice_fusion.2
  1188.8 1.1 constant_dynamic-slice_fusion.2
  1190.8 1.1 constant_dynamic-slice_fusion.2
  1192.9 1.1 constant_dynamic-slice_fusion.2
  1196.9 1.1 constant_dynamic-slice_fusion.2
  1198.9 1.1 constant_dynamic-slice_fusion.2
  1200.9 1.1 constant_dynamic-slice_fusion.2
  1205.0 1.1 constant_dynamic-slice_fusion.2
  1207.0 1.1 constant_dynamic-slice_fusion.2
  1209.0 1.1 constant_dynamic-slice_fusion.2
  1211.0 1.1 constant_dynamic-slice_fusion.2
  1215.0 1.1 constant_dynamic-slice_fusion.2
  1217.0 1.1 constant_dynamic-slice_fusion.2
  1219.1 1.1 constant_dynamic-slice_fusion.2
  1221.1 1.1 constant_dynamic-slice_fusion.2
  1247.3 1.1 constant_dynamic-slice_fusion.2
  1251.3 1.1 constant_dynamic-slice_fusion.2
  1275.5 1.1 constant_dynamic-slice_fusion.2
  1293.7 1.1 constant_dynamic-slice_fusion.2
  1301.7 1.1 constant_dynamic-slice_fusion.2
  1307.8 1.1 constant_dynamic-slice_fusion.2
  1319.9 1.1 constant_dynamic-slice_fusion.2
  1321.9 1.1 constant_dynamic-slice_fusion.2
  1326.0 1.1 constant_dynamic-slice_fusion.2
  1346.1 1.1 constant_dynamic-slice_fusion.2
  1348.1 1.1 constant_dynamic-slice_fusion.2
  1354.2 1.1 constant_dynamic-slice_fusion.2
  1370.3 1.1 constant_dynamic-slice_fusion.2
  1372.4 1.1 constant_dynamic-slice_fusion.2
  1378.4 1.1 constant_dynamic-slice_fusion.2
  1398.6 1.1 constant_dynamic-slice_fusion.2
  1400.6 1.1 constant_dynamic-slice_fusion.2
  1403.1 5.8 fusion.3
  1409.7 331.7 %all-gather.10.cloned.1.call-done = f32[131072,16]{0,1:T(8,128)} async-done(((f32[1024,16]{0,1:T(8,128)}), f32[131072,16]{0,1:T(8,128)}) %all-gather.10.cloned.1.call-update) | async-done | bytes 8388624 | tf_op jit(solution)/shard_map/all_gather | solution.py:14
  1741.4 8.3 copy.39
  1749.9 8.3 rev.7
  1758.2 8.5 rev.6
  1766.7 119.0 %while.29 = (s32[]{:T(128)}, f32[1024,16]{0,1:T(8,128)S(1)}, s32[]{:T(128)}, f32[128,1024,16]{1,2,0:T(8,128)}, f32[128,1024,16]{1,2,0:T(8,128)}, /*index=5*/s32[]{:T(128)}, s32[]{:T(128)}) while((s32[]{:T(128)}, f32[1024,16]{0,1:T(8,128)S(1)}, s32[]{:T(128)}, f32[128,1024,16]{1,2,0:T(8,128)}, f32[128,1024,16]{1,2,0:T(8,128)}, ...), condition=%wide.region_3.0_spmd.clone, body=%wide.region_2.0_spmd.clone.sunk | while | flops 65540 | bytes 262253 | solution.py:26
  1885.8 6.4 fusion.4
  1894.1 184.5 %psum.7 = f32[256,16]{0,1:T(8,128)} all-reduce(f32[256,16]{0,1:T(8,128)S(1)} %reduce_sum.169), channel_id=1, replica_groups=mesh['ctx'=128,'ch'=4] {'ctx','ch'}, use_global_device_ids=true, to_apply=%region_21.22 | all-reduce | flops 4096 | bytes 32768 | tf_op jit(solution)/shard_map/psum | solution.py:105
  (574 shorter events, 358.4 us)
Async XLA Ops:
  7.2 544.1 %all-gather.8.cloned.1.call-start = ((), (), s32[]{:S(2)}) async-start(), calls=%async_computation.1 | async-start | bytes 8454144 | tf_op jit(solution)/shard_map/all_gather | solution.py:14
  8.6 12.6 copy-start.69
  8.6 12.6 copy-start.70
  8.6 12.6 copy-start.71
  8.6 12.6 copy-start.72
  8.6 12.6 copy-start.73
  8.6 12.6 copy-start.74
  8.6 12.6 copy-start.75
  8.7 12.6 copy-start.76
  8.7 13.2 copy-start.77
  8.7 1394.3 %copy-start.35 = (f32[1024,1]{0,1:T(1,128)}, f32[1024,1]{0,1:T(1,128)S(1)}, u32[]{:S(2)}) copy-start(f32[1024,1]{0,1:T(1,128)S(1)} %get-tuple-element.342) | copy-start | bytes 12292
  8.7 1394.3 %copy-start.36 = (f32[1024,1]{0,1:T(1,128)}, f32[1024,1]{0,1:T(1,128)S(1)}, u32[]{:S(2)}) copy-start(f32[1024,1]{0,1:T(1,128)S(1)} %get-tuple-element.351) | copy-start | bytes 12292
  8.7 1394.3 %copy-start.38 = (f32[1024,1]{0,1:T(1,128)}, f32[1024,1]{0,1:T(1,128)S(1)}, u32[]{:S(2)}) copy-start(f32[1024,1]{0,1:T(1,128)S(1)} %get-tuple-element.343) | copy-start | bytes 12292
  8.7 1394.3 %copy-start.39 = (f32[1024,1]{0,1:T(1,128)}, f32[1024,1]{0,1:T(1,128)S(1)}, u32[]{:S(2)}) copy-start(f32[1024,1]{0,1:T(1,128)S(1)} %get-tuple-element.344) | copy-start | bytes 12292
  8.7 1394.3 %copy-start.40 = (f32[1024,1]{0,1:T(1,128)}, f32[1024,1]{0,1:T(1,128)S(1)}, u32[]{:S(2)}) copy-start(f32[1024,1]{0,1:T(1,128)S(1)} %get-tuple-element.345) | copy-start | bytes 12292
  8.7 1394.3 %copy-start.41 = (f32[1024,1]{0,1:T(1,128)}, f32[1024,1]{0,1:T(1,128)S(1)}, u32[]{:S(2)}) copy-start(f32[1024,1]{0,1:T(1,128)S(1)} %get-tuple-element.346) | copy-start | bytes 12292
  8.7 1394.3 %copy-start.42 = (f32[1024,1]{0,1:T(1,128)}, f32[1024,1]{0,1:T(1,128)S(1)}, u32[]{:S(2)}) copy-start(f32[1024,1]{0,1:T(1,128)S(1)} %get-tuple-element.347) | copy-start | bytes 12292
  8.7 1394.3 %copy-start.43 = (f32[1024,1]{0,1:T(1,128)}, f32[1024,1]{0,1:T(1,128)S(1)}, u32[]{:S(2)}) copy-start(f32[1024,1]{0,1:T(1,128)S(1)} %get-tuple-element.348) | copy-start | bytes 12292
  8.8 1394.3 %copy-start.44 = (f32[1024,1]{0,1:T(1,128)}, f32[1024,1]{0,1:T(1,128)S(1)}, u32[]{:S(2)}) copy-start(f32[1024,1]{0,1:T(1,128)S(1)} %get-tuple-element.349) | copy-start | bytes 12292
  8.8 12.5 copy-start.47
  8.8 12.5 copy-start.48
  8.8 12.5 copy-start.49
  8.8 12.5 copy-start.50
  8.8 12.5 copy-start.51
  8.8 12.5 copy-start.52
  8.9 12.5 copy-start.46
  14.4 9.8 copy-start.25
  14.9 9.2 copy-start.26
  15.5 8.7 copy-start.27
  16.1 8.1 copy-start.28
  16.6 7.8 copy-start.29
  16.6 9.7 copy-start.45
  17.2 7.2 copy-start.30
  17.8 6.7 copy-start.31
  20.0 4.2 copy-start
  20.6 3.8 copy-start.1
  21.3 3.1 copy-start.2
  24.3 1378.8 %copy-start.37 = (f32[1024,1]{0,1:T(1,128)}, f32[1024,1]{0,1:T(1,128)S(1)}, u32[]{:S(2)}) copy-start(f32[1024,1]{0,1:T(1,128)S(1)} %get-tuple-element.320) | copy-start | bytes 12292
  24.4 1378.7 %copy-start.34 = (f32[1024,1]{0,1:T(1,128)}, f32[1024,1]{0,1:T(1,128)S(1)}, u32[]{:S(2)}) copy-start(f32[1024,1]{0,1:T(1,128)S(1)} %get-tuple-element.341) | copy-start | bytes 12292
  26.3 1120.2 %all-gather.6.cloned.1.call-start = ((), (), s32[]{:S(2)}) async-start(), calls=%async_computation | async-start | bytes 8454144 | tf_op jit(solution)/shard_map/all_gather | solution.py:14
  27.1 1714.4 %all-gather.10.cloned.1.call-start = ((), (), s32[]{:S(2)}) async-start(), calls=%async_computation.2 | async-start | bytes 8454144 | tf_op jit(solution)/shard_map/all_gather | solution.py:14
  34.1 20.7 copy-start.78
  551.3 851.4 %copy-start.32 = (f32[1024,16]{0,1:T(8,128)S(1)}, f32[1024,16]{0,1:T(8,128)}, u32[]{:S(2)}) copy-start(f32[1024,16]{0,1:T(8,128)} %stack.74) | copy-start | bytes 196612
  1402.8 347.0 %copy-start.53 = (f32[1024,1]{0,1:T(1,128)}, f32[1024,1]{0,1:T(1,128)S(1)}, u32[]{:S(2)}) copy-start(f32[1024,1]{0,1:T(1,128)S(1)} %get-tuple-element.304) | copy-start | bytes 12292
  1402.8 346.9 %copy-start.54 = (f32[1024,1]{0,1:T(1,128)}, f32[1024,1]{0,1:T(1,128)S(1)}, u32[]{:S(2)}) copy-start(f32[1024,1]{0,1:T(1,128)S(1)} %get-tuple-element.305) | copy-start | bytes 12292
  1402.8 346.9 %copy-start.55 = (f32[1024,1]{0,1:T(1,128)}, f32[1024,1]{0,1:T(1,128)S(1)}, u32[]{:S(2)}) copy-start(f32[1024,1]{0,1:T(1,128)S(1)} %get-tuple-element.306) | copy-start | bytes 12292
  1402.8 346.9 %copy-start.56 = (f32[1024,1]{0,1:T(1,128)}, f32[1024,1]{0,1:T(1,128)S(1)}, u32[]{:S(2)}) copy-start(f32[1024,1]{0,1:T(1,128)S(1)} %get-tuple-element.307) | copy-start | bytes 12292
  1402.8 346.9 %copy-start.57 = (f32[1024,1]{0,1:T(1,128)}, f32[1024,1]{0,1:T(1,128)S(1)}, u32[]{:S(2)}) copy-start(f32[1024,1]{0,1:T(1,128)S(1)} %get-tuple-element.308) | copy-start | bytes 12292
  1402.9 346.9 %copy-start.58 = (f32[1024,1]{0,1:T(1,128)}, f32[1024,1]{0,1:T(1,128)S(1)}, u32[]{:S(2)}) copy-start(f32[1024,1]{0,1:T(1,128)S(1)} %get-tuple-element.309) | copy-start | bytes 12292
  1402.9 346.9 %copy-start.59 = (f32[1024,1]{0,1:T(1,128)}, f32[1024,1]{0,1:T(1,128)S(1)}, u32[]{:S(2)}) copy-start(f32[1024,1]{0,1:T(1,128)S(1)} %get-tuple-element.310) | copy-start | bytes 12292
  1402.9 346.9 %copy-start.60 = (f32[1024,1]{0,1:T(1,128)}, f32[1024,1]{0,1:T(1,128)S(1)}, u32[]{:S(2)}) copy-start(f32[1024,1]{0,1:T(1,128)S(1)} %get-tuple-element.311) | copy-start | bytes 12292
  1402.9 346.9 %copy-start.61 = (f32[1024,1]{0,1:T(1,128)}, f32[1024,1]{0,1:T(1,128)S(1)}, u32[]{:S(2)}) copy-start(f32[1024,1]{0,1:T(1,128)S(1)} %get-tuple-element.312) | copy-start | bytes 12292
  1402.9 346.9 %copy-start.62 = (f32[1024,1]{0,1:T(1,128)}, f32[1024,1]{0,1:T(1,128)S(1)}, u32[]{:S(2)}) copy-start(f32[1024,1]{0,1:T(1,128)S(1)} %get-tuple-element.313) | copy-start | bytes 12292
  1402.9 346.9 %copy-start.63 = (f32[1024,1]{0,1:T(1,128)}, f32[1024,1]{0,1:T(1,128)S(1)}, u32[]{:S(2)}) copy-start(f32[1024,1]{0,1:T(1,128)S(1)} %get-tuple-element.314) | copy-start | bytes 12292
  1402.9 346.9 %copy-start.64 = (f32[1024,1]{0,1:T(1,128)}, f32[1024,1]{0,1:T(1,128)S(1)}, u32[]{:S(2)}) copy-start(f32[1024,1]{0,1:T(1,128)S(1)} %get-tuple-element.315) | copy-start | bytes 12292
  1402.9 346.9 %copy-start.65 = (f32[1024,1]{0,1:T(1,128)}, f32[1024,1]{0,1:T(1,128)S(1)}, u32[]{:S(2)}) copy-start(f32[1024,1]{0,1:T(1,128)S(1)} %get-tuple-element.316) | copy-start | bytes 12292
  1402.9 346.9 %copy-start.66 = (f32[1024,1]{0,1:T(1,128)}, f32[1024,1]{0,1:T(1,128)S(1)}, u32[]{:S(2)}) copy-start(f32[1024,1]{0,1:T(1,128)S(1)} %get-tuple-element.317) | copy-start | bytes 12292
  1402.9 346.9 %copy-start.67 = (f32[1024,1]{0,1:T(1,128)}, f32[1024,1]{0,1:T(1,128)S(1)}, u32[]{:S(2)}) copy-start(f32[1024,1]{0,1:T(1,128)S(1)} %get-tuple-element.318) | copy-start | bytes 12292
  1403.0 346.9 %copy-start.68 = (f32[1024,1]{0,1:T(1,128)}, f32[1024,1]{0,1:T(1,128)S(1)}, u32[]{:S(2)}) copy-start(f32[1024,1]{0,1:T(1,128)S(1)} %get-tuple-element.319) | copy-start | bytes 12292
  1758.2 127.6 %copy-start.5 = (f32[1024,128]{0,1:T(8,128)S(1)}, f32[1024,128]{0,1:T(8,128)}, u32[]{:S(2)}) copy-start(f32[1024,128]{0,1:T(8,128)} %copy-done.4) | copy-start | bytes 1572868
  1758.2 127.6 %copy-start.7 = (f32[1024,128]{0,1:T(8,128)S(1)}, f32[1024,128]{0,1:T(8,128)}, u32[]{:S(2)}) copy-start(f32[1024,128]{0,1:T(8,128)} %copy-done.6) | copy-start | bytes 1572868
  1758.2 127.6 %copy-start.9 = (f32[1024,128]{0,1:T(8,128)S(1)}, f32[1024,128]{0,1:T(8,128)}, u32[]{:S(2)}) copy-start(f32[1024,128]{0,1:T(8,128)} %copy-done.8) | copy-start | bytes 1572868
  1758.2 127.6 %copy-start.11 = (f32[1024,128]{0,1:T(8,128)S(1)}, f32[1024,128]{0,1:T(8,128)}, u32[]{:S(2)}) copy-start(f32[1024,128]{0,1:T(8,128)} %copy-done.10) | copy-start | bytes 1572868
  1758.2 127.6 %copy-start.13 = (f32[1024,128]{0,1:T(8,128)S(1)}, f32[1024,128]{0,1:T(8,128)}, u32[]{:S(2)}) copy-start(f32[1024,128]{0,1:T(8,128)} %copy-done.12) | copy-start | bytes 1572868
  (18 other events, 16.2 us)
Sparse Core Ops, SparseCore 0:
  26.4 524.8 all-gather.7
  553.9 592.4 all-gather.5
  1148.6 592.8 all-gather.9
where the time goes:
time: 2110 us; the launch traced here: 2090 us
  waiting for transfers between devices  1410 us (67%)
  other arithmetic  246 us (12%)
  local copies, waits for them, and re-layouts  201 us (10%)
  blocking collectives  185 us (9%)
    all_gather x3, waiting for transfers between devices, entering(): pieces = jax.tree.map(lambda part: lax.all_gather(part, axis), value)  1410 us
    select_n x254, other arithmetic, hop(): jnp.where(position < mine, new, old)  230 us
    psum x1, blocking collectives, local(): grad_residue = lax.psum(grouped, ('ctx', 'ch'))  185 us
    dynamic_slice x127, local copies, waits for them, and re-layouts, hop(): longer = join(running, jax.tree.map(lambda part: part[position], pieces))  139 us
  transfers between devices with their start and end apart: 3, of which 3 were waited for; matrix products, arithmetic and copies ran while one was open for 14% of the time, Pallas kernels for 0%

commit v1 on v0

v1 whole, which is shorter than its diff:
```python
import functools
import math

import jax
import jax.numpy as jnp
from jax import lax
from jax.experimental import pallas as pl
from jax.experimental.pallas import tpu as pltpu
from jax.sharding import PartitionSpec as P

MESH = pl.DeviceIdType.MESH
F32 = jnp.float32

NX, NZ, NY, NCH = 4, 16, 2, 4
PLANE = NX * NY
MODES = 16
FG = 256
CHN = 1024
ROWS = 128
SUB = 8
GROUP = 8
BACK = (-4, 3, -3, 2, -2, 1, -1)
ACROSS = (8, 7, 9, 6, 10, 5, 11, 4, 12, 3, 13, 2, 14, 1, 15)
IN_PLANE = (6, 2, 5, 7, 3, 1, 4)


def tree_sum(terms):
    terms = list(terms)
    while len(terms) > 1:
        terms = [
            terms[i] + terms[i + 1] if i + 1 < len(terms) else terms[i]
            for i in range(0, len(terms), 2)
        ]
    return terms[0]


def scan_kernel(
    norm,
    q_hbm, k_hbm, v_hbm, g_hbm, rate_hbm, resid_hbm,
    gq_out, gk_out, gv_out, res_out,
    q_in, k_in, v_in, g_in, rate_in, resid_in,
    x_kv, x_g, c_out, c_grad,
    d_tab, w_tab, plane_decay_tab, block_decay_tab,
    a_send, a_recv, tot, b_send, b_recv, owner_out, c_recv, grp, e_send, e_recv,
    ch_recv, f_send, f_recv, in_sem, send_sem, recv_sem,
):
    ctx, ch = lax.axis_index("ctx"), lax.axis_index("ch")
    x, z, y = ctx % NX, (ctx // NX) % NZ, ctx // (NX * NZ)
    a = y * NX + x

    def plane_id(p):
        return ((p // NX) * NZ + z) * NX + p % NX, ch

    def z_id(zz):
        return (y * NZ + zz) * NX + x, ch

    plane = [(a + k) % PLANE for k in IN_PLANE]
    across = [(z + k) % NZ for k in ACROSS]
    others = [(ch + k) % NCH for k in range(1, NCH)]

    loads = [
        pltpu.make_async_copy(src, dst, in_sem.at[i])
        for i, (src, dst) in enumerate(
            [
                (k_hbm, k_in), (v_hbm, v_in), (g_hbm, g_in), (q_hbm, q_in),
                (rate_hbm, rate_in), (resid_hbm, resid_in),
            ]
        )
    ]
    for load in loads:
        load.start()

    barrier = pltpu.get_barrier_semaphore()
    for zz in across:
        pl.semaphore_signal(barrier, inc=1, device_id=z_id(zz), device_id_type=MESH)
    for p in plane:
        pl.semaphore_signal(barrier, inc=1, device_id=plane_id(p), device_id_type=MESH)
    for c in others:
        pl.semaphore_signal(barrier, inc=1, device_id=(ctx, c), device_id_type=MESH)

    loads[4].wait()
    loads[5].wait()
    rate_t = rate_in[...]
    weight_t = resid_in[...] * jnp.sqrt(2.0 * rate_t)
    odd = lax.broadcasted_iota(jnp.int32, (SUB, ROWS), 0) % 2 == 1
    for m in range(MODES):
        rate = jnp.where(odd, rate_t[m : m + 1, ROWS:], rate_t[m : m + 1, :ROWS])
        d_tab[m] = jnp.exp(-rate)
        block_decay_tab[m] = jnp.exp(-rate * ROWS)
        plane_decay_tab[m] = jnp.exp(-rate * (ROWS * NX))
        w_tab[m] = jnp.where(odd, weight_t[m : m + 1, ROWS:], weight_t[m : m + 1, :ROWS])

    loads[0].wait()
    loads[1].wait()
    for j in range(SUB):
        rows = pl.ds(j * ROWS, ROWS)
        product = k_in[rows, :].astype(F32) * v_in[rows, :].astype(F32)
        x_kv[pl.ds(j, ROWS, stride=SUB), :] = product.T
    loads[2].wait()
    loads[3].wait()
    for j in range(SUB):
        rows = pl.ds(j * ROWS, ROWS)
        product = g_in[rows, :].astype(F32) * q_in[rows, :].astype(F32)
        x_g[pl.ds(j, ROWS, stride=SUB), :] = product.T

    def at(t):
        return pl.ds(pl.multiple_of(t * SUB, SUB), SUB)

    zero = jnp.zeros((SUB, ROWS), F32)
    for first in range(0, MODES, GROUP):
        modes = range(first, first + GROUP)
        d = [d_tab[m] for m in modes]
        w = [w_tab[m] for m in modes]

        def local_step(t, carry, d=d, w=w, first=first):
            ahead, back, acc = carry
            here, there = at(t), at(ROWS - 1 - t)
            value, grad, late = x_kv[here, :], x_g[here, :], x_g[there, :]
            ahead = tuple(d[i] * ahead[i] + value for i in range(GROUP))
            back = tuple(d[i] * back[i] + late for i in range(GROUP))
            acc = tuple(acc[i] + grad * ahead[i] for i in range(GROUP))
            out = tree_sum(w[i] * ahead[i] for i in range(GROUP))
            out_grad = tree_sum(w[i] * back[i] for i in range(GROUP))
            if first:
                out = out + c_out[here, :]
                out_grad = out_grad + c_grad[there, :]
            c_out[here, :] = out
            c_grad[there, :] = out_grad
            return ahead, back, acc

        start = ((zero,) * GROUP,) * 3
        ahead, back, acc = lax.fori_loop(0, ROWS, local_step, start, unroll=4)
        for i, m in enumerate(modes):
            a_send[m // 2, m % 2] = ahead[i]
            a_send[m // 2, 2 + m % 2] = back[i]
            a_send[m // 2, 4 + m % 2] = acc[i]

    pl.semaphore_wait(barrier, len(plane) + len(across) + len(others))

    sent = []

    def send(src, dst, sem, device):
        copy = pltpu.make_async_remote_copy(
            src_ref=src, dst_ref=dst, send_sem=send_sem.at[sem], recv_sem=recv_sem.at[sem],
            device_id=device, device_id_type=MESH,
        )
        copy.start()
        sent.append(copy)
        return copy

    copies = [
        send(a_send.at[p], a_recv.at[a], i, plane_id(p)) for i, p in enumerate(plane)
    ]
    a_recv[a] = a_send[a]
    mine = pl.ds(2 * a, 2)
    d2, block_decay, plane_decay = d_tab[mine], block_decay_tab[mine], plane_decay_tab[mine]
    for copy in copies:
        copy.wait_recv()

    resid = jnp.zeros((2, SUB, ROWS), F32)
    for yy in range(NY):
        run = jnp.zeros((2, SUB, ROWS), F32)
        for xx in range(NX):
            slot = yy * NX + xx
            resid = resid + a_recv[slot, 4:6] + d2 * a_recv[slot, 2:4] * run
            run = block_decay * run + a_recv[slot, 0:2]
        tot[yy] = run
        run = jnp.zeros((2, SUB, ROWS), F32)
        for xx in reversed(range(NX)):
            run = block_decay * run + a_recv[yy * NX + xx, 2:4]
        tot[2 + yy] = run
    tot[4] = resid
    tot[5] = plane_decay
    tot[6] = d2

    for p in range(SUB):
        for item in range(5):
            b_send[p, item] = tot[item, p // 4, 2 * (p % 4) : 2 * (p % 4) + 2, :]
    base = len(plane)
    copies = [
        send(b_send.at[zz % SUB], b_recv.at[z], base + i, z_id(zz)) for i, zz in enumerate(across)
    ]
    b_recv[z] = b_send[z % SUB]
    pair = z % SUB
    decay_rows = tot_rows(tot, 5, pair)
    step_rows = tot_rows(tot, 6, pair)
    for copy in copies:
        copy.wait_recv()

    run = jnp.zeros((2, ROWS), F32)
    total = jnp.zeros((2, ROWS), F32)
    for yy in range(NY):
        for zz in range(NZ):
            owner_out[zz, yy] = run
            total = total + step_rows * b_recv[zz, 2 + yy] * run
            run = decay_rows * run + b_recv[zz, yy]
    run = jnp.zeros((2, ROWS), F32)
    for yy in reversed(range(NY)):
        for zz in reversed(range(NZ)):
            owner_out[zz, 2 + yy] = run
            run = decay_rows * run + b_recv[zz, 2 + yy]
    for zz in range(NZ):
        total = total + b_recv[zz, 4]
    for zz in range(NZ):
        owner_out[zz, 4] = total

    base += len(across)
    copies = [
        send(owner_out.at[(z + k) % NZ], c_recv.at[pair], base + i, z_id((z + k) % NZ))
        for i, k in enumerate(BACK)
    ]
    c_recv[pair] = owner_out[z]
    for copy in copies:
        copy.wait_recv()

    for i in range(2):
        ch_recv[ch, i] = (c_recv[4 * i, 4] + c_recv[4 * i + 1, 4]) + (
            c_recv[4 * i + 2, 4] + c_recv[4 * i + 3, 4]
        )
    base += len(BACK)
    ch_copies = [
        send(ch_recv.at[ch], ch_recv.at[ch], base + i, (ctx, c)) for i, c in enumerate(others)
    ]

    for p in range(SUB):
        for item in range(4):
            grp[item, p // 4, 2 * (p % 4) : 2 * (p % 4) + 2, :] = c_recv[p, item]
    for yy in range(NY):
        run = grp[yy]
        for xx in range(NX):
            slot = yy * NX + xx
            e_send[slot, 0:2] = run
            run = block_decay * run + a_recv[slot, 0:2]
        run = grp[2 + yy]
        for xx in reversed(range(NX)):
            slot = yy * NX + xx
            e_send[slot, 2:4] = run
            run = block_decay * run + a_recv[slot, 2:4]
    base += len(others)
    copies = [
        send(e_send.at[p], e_recv.at[a], base + i, plane_id(p)) for i, p in enumerate(plane)
    ]
    e_recv[a] = e_send[a]
    base += len(plane)

    for copy in ch_copies:
        copy.wait_recv()
    f_send[...] = (ch_recv[0] + ch_recv[1]) + (ch_recv[2] + ch_recv[3])
    f_copies = [send(f_send, f_recv.at[a], base + i, plane_id(p)) for i, p in enumerate(plane)]
    f_recv[a] = f_send[...]

    for copy in copies:
        copy.wait_recv()

    d = [d_tab[m] for m in range(MODES)]
    w = [w_tab[m] for m in range(MODES)]
    ahead = tuple(w[m] * e_recv[m // 2, m % 2] for m in range(MODES))
    back = tuple(w[m] * e_recv[m // 2, 2 + m % 2] for m in range(MODES))

    def carry_step(t, carry):
        ahead, back = carry
        here, there = at(t), at(ROWS - 1 - t)
        ahead = tuple(d[m] * ahead[m] for m in range(MODES))
        back = tuple(d[m] * back[m] for m in range(MODES))
        c_out[here, :] = c_out[here, :] + tree_sum(ahead)
        c_grad[there, :] = c_grad[there, :] + tree_sum(back)
        return ahead, back

    lax.fori_loop(0, ROWS, carry_step, (ahead, back), unroll=4)

    for j in range(SUB):
        rows = pl.ds(j * ROWS, ROWS)
        lanes = pl.ds(j, ROWS, stride=SUB)
        gq_out[rows, :] = (g_in[rows, :].astype(F32) * c_out[lanes, :].T).astype(jnp.bfloat16)
        conv_grad = c_grad[lanes, :].T
        gk_out[rows, :] = (conv_grad * v_in[rows, :].astype(F32)).astype(jnp.bfloat16)
        gv_out[rows, :] = (conv_grad * k_in[rows, :].astype(F32)).astype(jnp.bfloat16)

    for copy in f_copies:
        copy.wait_recv()
    for m in range(MODES):
        for odd_half in range(2):
            cols = pl.ds(odd_half * ROWS, ROWS)
            res_out[m : m + 1, cols] = f_recv[m // 2, m % 2, odd_half : odd_half + 1, :]
    res_out[...] = res_out[...] * (jnp.sqrt(2.0 * rate_in[...]) * norm)
    for copy in sent:
        copy.wait_send()


def tot_rows(tot, item, pair):
    rows = jnp.zeros((2, ROWS), F32)
    for p in range(SUB):
        piece = tot[item, p // 4, 2 * (p % 4) : 2 * (p % 4) + 2, :]
        rows = jnp.where(pair == p, piece, rows)
    return rows


def scan_call(norm, q, k, v, g, rates, residue):
    hbm = pl.BlockSpec(memory_space=pltpu.HBM)
    vmem = pl.BlockSpec(memory_space=pltpu.VMEM)
    big = pltpu.VMEM((CHN, ROWS), F32)
    half = pltpu.VMEM((CHN, ROWS), jnp.bfloat16)
    table = pltpu.VMEM((MODES, SUB, ROWS), F32)
    small = pltpu.VMEM((MODES, FG), F32)
    copies = 3 * (PLANE - 1) + NZ - 1 + len(BACK) + NCH - 1
    wide = jax.ShapeDtypeStruct((CHN, ROWS), jnp.bfloat16)
    return pl.pallas_call(
        functools.partial(scan_kernel, norm),
        out_shape=(wide, wide, wide, jax.ShapeDtypeStruct((MODES, FG), F32)),
        in_specs=[hbm] * 6,
        out_specs=(vmem,) * 4,
        scratch_shapes=[
            half, half, half, half, small, small,
            big, big, big, big,
            table, table, table, table,
            pltpu.VMEM((PLANE, 6, SUB, ROWS), F32),
            pltpu.VMEM((PLANE, 6, SUB, ROWS), F32),
            pltpu.VMEM((7, 2, SUB, ROWS), F32),
            pltpu.VMEM((SUB, 5, 2, ROWS), F32),
            pltpu.VMEM((NZ, 5, 2, ROWS), F32),
            pltpu.VMEM((NZ, 5, 2, ROWS), F32),
            pltpu.VMEM((SUB, 5, 2, ROWS), F32),
            pltpu.VMEM((4, 2, SUB, ROWS), F32),
            pltpu.VMEM((PLANE, 4, SUB, ROWS), F32),
            pltpu.VMEM((PLANE, 4, SUB, ROWS), F32),
            pltpu.VMEM((NCH, 2, 2, ROWS), F32),
            pltpu.VMEM((2, 2, ROWS), F32),
            pltpu.VMEM((PLANE, 2, 2, ROWS), F32),
            pltpu.SemaphoreType.DMA((6,)),
            pltpu.SemaphoreType.DMA((copies,)),
            pltpu.SemaphoreType.DMA((copies,)),
        ],
        compiler_params=pltpu.CompilerParams(
            collective_id=0, has_side_effects=True, vmem_limit_bytes=63 * 2**20
        ),
        name="scan_states",
    )(q, k, v, g, rates, residue)


def finish_kernel(*refs):
    half = (len(refs) - 2) // 3
    srcs, dsts, held = refs[:half], refs[half : 2 * half], refs[2 * half : 3 * half]
    in_sem, out_sem = refs[3 * half :]
    loads = [pltpu.make_async_copy(srcs[i], held[i], in_sem.at[i]) for i in range(half)]
    stores = [pltpu.make_async_copy(held[i], dsts[i], out_sem.at[i]) for i in range(half)]
    for load in loads:
        load.start()
    for load, store in zip(loads, stores):
        load.wait()
        store.start()
    for store in stores:
        store.wait()


def finish_call(*results):
    n = len(results)
    hbm = pl.BlockSpec(memory_space=pl.ANY)
    return pl.pallas_call(
        finish_kernel,
        out_shape=tuple(jax.ShapeDtypeStruct(r.shape, r.dtype) for r in results),
        in_specs=[hbm] * n,
        out_specs=(hbm,) * n,
        scratch_shapes=[pltpu.VMEM(r.shape, r.dtype) for r in results]
        + [pltpu.SemaphoreType.DMA((n,)), pltpu.SemaphoreType.DMA((n,))],
        name="finish",
    )(*results)


def local(q_branch, k_branch, v_branch, grad_gated, decay_rates, residue):
    norm = 1.0 / math.sqrt(q_branch.shape[1] * lax.axis_size("ctx"))
    grad_q, grad_k, grad_v, res = finish_call(
        *scan_call(norm, q_branch, k_branch, v_branch, grad_gated, decay_rates.T, residue.T)
    )
    return grad_q, grad_k, grad_v, res.T


def solution(mesh):
    in_specs = (P("ch", "ctx"), P("ch", "ctx"), P("ch", "ctx"), P("ch", "ctx"), P(), P())
    out_specs = (P("ch", "ctx"), P("ch", "ctx"), P("ch", "ctx"), P())
    return jax.shard_map(local, mesh=mesh, in_specs=in_specs, out_specs=out_specs, check_vma=False)
```

time: 2110 us -> 44.2 us (0.02); the launches traced: 2090 us -> 44.1 us
  waiting for transfers between devices: 1410 us -> 0 us
  other arithmetic: 246 us -> 0 us
  local copies, waits for them, and re-layouts: 201 us -> 0 us
  blocking collectives: 185 us -> 0 us
  Pallas kernels: 0 us -> 43.4 us
    all_gather x3 -> x0, waiting for transfers between devices: 1410 us -> none  [entering(): pieces = jax.tree.map(lambda part: lax.all_gather(part, axis), value)]
    select_n x254 -> x0, other arithmetic: 230 us -> none  [hop(): jnp.where(position < mine, new, old)]
    psum x1 -> x0, blocking collectives: 185 us -> none  [local(): grad_residue = lax.psum(grouped, ('ctx', 'ch'))]
    dynamic_slice x127 -> x0, local copies, waits for them, and re-layouts: 139 us -> none  [hop(): longer = join(running, jax.tree.map(lambda part: part[position], pieces))]
    pallas_call x0 -> x2, Pallas kernels: none -> 43.4 us  [the longest x1 41.5 us: scan_call(): pl.pallas_call(functools.partial(scan_kernel, norm), out_shape=(wide, wid...]
    unnamed x168 -> x0, local copies, waits for them, and re-layouts: 32.1 us -> none
  transfers between devices with their start and end apart: 3 -> 0, of which waited for: 3 -> 0; matrix products, arithmetic and copies ran while one was open for 14% -> 0% of each run, Pallas kernels for 0% -> 0%
where the time goes in v1:
time: 44.2 us; the launch traced here: 44.1 us
  Pallas kernels  43.4 us (98%)
  between operations  0.64 us (1%)
    pallas_call x1, Pallas kernels, scan_call(): pl.pallas_call(functools.partial(scan_kernel, norm), out_shape=(wide, wid...  41.5 us
    pallas_call x1, Pallas kernels, finish_call(): pl.pallas_call(finish_kernel, out_shape=tuple((jax.ShapeDtypeStruct(r.sha...  1.9 us

profile of v1, /device:TPU:1, one launch (start us, length us, event | category | flops | bytes accessed | tf_op | source)
XLA Modules:
  0.0 44.1 jit_solution(12587909283808164252)
XLA Ops:
  0.6 41.5 %scan_states.1 = (bf16[1024,128]{1,0:T(8,128)(2,1)}, bf16[1024,128]{1,0:T(8,128)(2,1)}, bf16[1024,128]{1,0:T(8,128)(2,1)}, f32[16,256]{1,0:T(8,128)}) custom-call(bf16[1024,128]{1,0:T(8,128)(2,1)} %q_hbm.1, bf16[1024,128]{1,0:T(8,128)(2,1)} %k_hbm.1, bf16[1024,128]{1,0:T(8,128)(2,1)} %v_hbm.1, bf16[1024,128]{1,0:T(8,128)(2,1)} %g_hbm.1, f32[16,256]{1,0:T(8,128)} %bitcast.3, ...), custom_call_target="tpu_custom_call" | custom-call | tf_op jit(solution)/shard_map/scan_states/pallas_call | solution.py:307
  42.2 1.9 %finish.1 = (bf16[1024,128]{1,0:T(8,128)(2,1)}, bf16[1024,128]{1,0:T(8,128)(2,1)}, bf16[1024,128]{1,0:T(8,128)(2,1)}, f32[16,256]{1,0:T(8,128)}) custom-call(bf16[1024,128]{1,0:T(8,128)(2,1)} %get-tuple-element.12.refs_0_, bf16[1024,128]{1,0:T(8,128)(2,1)} %get-tuple-element.13.refs_1_, bf16[1024,128]{1,0:T(8,128)(2,1)} %get-tuple-element.14.refs_2_, ...), custom_call_target="tpu_custom_call" | custom-call | tf_op jit(solution)/shard_map/finish/pallas_call | solution.py:358

commit v2 on v1

v2 whole, which is shorter than its diff:
```python
import functools
import math

import jax
import jax.numpy as jnp
from jax import lax
from jax.experimental import pallas as pl
from jax.experimental.pallas import tpu as pltpu
from jax.sharding import PartitionSpec as P

MESH = pl.DeviceIdType.MESH
F32 = jnp.float32

NX, NZ, NY, NCH = 4, 16, 2, 4
PLANE = NX * NY
MODES = 16
FG = 256
CHN = 1024
ROWS = 128
SUB = 8
GROUP = 8
HOME = 0
ANSWER_FIRST = (1, 2, 3)
ANSWER_LATER = (4, 5, 6, 7, 15, 8, 14, 9, 13, 10, 12, 11)
NEAR = ((0, 1), (0, 3), (1, 0))
FAR = ((1, 2), (1, 1), (1, 3), (0, 2))


def tree_sum(terms):
    terms = list(terms)
    while len(terms) > 1:
        terms = [
            terms[i] + terms[i + 1] if i + 1 < len(terms) else terms[i]
            for i in range(0, len(terms), 2)
        ]
    return terms[0]


def scan_kernel(
    norm,
    q_hbm, k_hbm, v_hbm, g_hbm, rate_hbm, resid_hbm,
    gq_hbm, gk_hbm, gv_hbm, res_out,
    q_in, k_in, v_in, g_in, rate_in, resid_in,
    x_kv, x_g, c_out, c_grad, gq_out, gk_out, gv_out,
    d_tab, w_tab, plane_decay_tab, block_decay_tab,
    a_send, a_recv, rows_tmp, b_send, b_recv, owner_out, c_recv, r_send, r_recv, e_send, e_recv,
    f_send, f_recv, in_sem, out_sem,
    a_send_sem, a_recv_sem, b_send_sem, b_recv_sem, c_send_sem, c_recv_sem,
    r_send_sem, r_recv_sem, e_send_sem, e_recv_sem, f_send_sem, f_recv_sem,
):
    ctx, ch = lax.axis_index("ctx"), lax.axis_index("ch")
    y, z, x = lax.div(ctx, NX * NZ), lax.rem(lax.div(ctx, NX), NZ), lax.rem(ctx, NX)
    a = y * NX + x
    is_home = z == HOME
    x_plus = [lax.rem(x + k, NX) for k in range(NX)]
    y_plus = [lax.rem(y + k, NY) for k in range(NY)]
    ch_plus = [lax.rem(ch + k, NCH) for k in range(NCH)]
    column = y * (NZ * NX) + x

    plane = [y_plus[dy] * NX + x_plus[dx] for dy, dx in FAR + NEAR]
    plane_ids = [((y_plus[dy] * NZ + z) * NX + x_plus[dx], ch) for dy, dx in FAR + NEAR]

    def z_id(zz, dch=0):
        return column + zz * NX, ch_plus[dch]

    loads = [
        pltpu.make_async_copy(src, dst, in_sem.at[i])
        for i, (src, dst) in enumerate(
            [
                (k_hbm, k_in), (v_hbm, v_in), (g_hbm, g_in), (q_hbm, q_in),
                (rate_hbm, rate_in), (resid_hbm, resid_in),
            ]
        )
    ]
    for i in (4, 5, 0, 1, 2, 3):
        loads[i].start()

    barrier = pltpu.get_barrier_semaphore()

    def greet(device):
        pl.semaphore_signal(barrier, inc=1, device_id=device, device_id_type=MESH)

    for device in plane_ids:
        greet(device)

    @pl.when(jnp.logical_not(is_home))
    def _():
        for k in range(NCH):
            greet(z_id(HOME, k))

    @pl.when(is_home)
    def _():
        for k in range(1, NCH):
            greet(z_id(HOME, k))

        @pl.loop(0, NZ)
        def _(zz):
            @pl.when(zz != HOME)
            def _():
                for k in range(NCH):
                    greet(z_id(zz, k))

    loads[4].wait()
    loads[5].wait()
    rate_t = rate_in[...]
    weight_t = resid_in[...] * jnp.sqrt(2.0 * rate_t)
    odd = lax.broadcasted_iota(jnp.int32, (SUB, ROWS), 0) % 2 == 1
    for m in range(MODES):
        rate = jnp.where(odd, rate_t[m : m + 1, ROWS:], rate_t[m : m + 1, :ROWS])
        d_tab[m] = jnp.exp(-rate)
        block_decay_tab[m] = jnp.exp(-rate * ROWS)
        plane_decay_tab[m] = jnp.exp(-rate * (ROWS * NX))
        w_tab[m] = jnp.where(odd, weight_t[m : m + 1, ROWS:], weight_t[m : m + 1, :ROWS])

    loads[0].wait()
    loads[1].wait()
    for j in range(SUB):
        rows = pl.ds(j * ROWS, ROWS)
        product = k_in[rows, :].astype(F32) * v_in[rows, :].astype(F32)
        x_kv[pl.ds(j, ROWS, stride=SUB), :] = product.T
    loads[2].wait()
    loads[3].wait()
    for j in range(SUB):
        rows = pl.ds(j * ROWS, ROWS)
        product = g_in[rows, :].astype(F32) * q_in[rows, :].astype(F32)
        x_g[pl.ds(j, ROWS, stride=SUB), :] = product.T

    def at(t):
        return pl.ds(pl.multiple_of(t * SUB, SUB), SUB)

    zero = jnp.zeros((SUB, ROWS), F32)
    for p in range(PLANE):
        a_send[p, 4] = zero
    for first in range(0, MODES, GROUP):
        modes = range(first, first + GROUP)
        d = [d_tab[m] for m in modes]

        def end_step(t, carry, d=d):
            ahead, back, acc = carry
            here, there = at(t), at(ROWS - 1 - t)
            value, grad, late = x_kv[here, :], x_g[here, :], x_g[there, :]
            ahead = tuple(d[i] * ahead[i] + value for i in range(GROUP))
            back = tuple(d[i] * back[i] + late for i in range(GROUP))
            acc = tuple(acc[i] + grad * ahead[i] for i in range(GROUP))
            return ahead, back, acc

        start = ((zero,) * GROUP,) * 3
        ahead, back, acc = lax.fori_loop(0, ROWS, end_step, start, unroll=4)
        for i, m in enumerate(modes):
            a_send[m // 2, m % 2] = ahead[i]
            a_send[m // 2, 2 + m % 2] = back[i]
            rows = 2 * (m % 2)
            a_send[m // 2, 4, rows : rows + 2, :] = tree_sum(
                acc[i][2 * r : 2 * r + 2, :] for r in range(4)
            )

    pl.semaphore_wait(barrier, len(plane) + jnp.where(is_home, NZ * NCH - 1, NCH))

    def remote(src, dst, send_sem, recv_sem, device):
        return pltpu.make_async_remote_copy(
            src_ref=src, dst_ref=dst, send_sem=send_sem, recv_sem=recv_sem,
            device_id=device, device_id_type=MESH,
        )

    a_copies = [
        remote(a_send.at[p], a_recv.at[a], a_send_sem.at[i], a_recv_sem.at[i], device)
        for i, (p, device) in enumerate(zip(plane, plane_ids))
    ]
    for copy in a_copies:
        copy.start()
    a_recv[a] = a_send[a]

    for first in range(0, MODES, GROUP):
        modes = range(first, first + GROUP)
        d = [d_tab[m] for m in modes]
        w = [w_tab[m] for m in modes]

        def local_step(t, carry, d=d, w=w, first=first):
            ahead, back = carry
            here, there = at(t), at(ROWS - 1 - t)
            value, late = x_kv[here, :], x_g[there, :]
            ahead = tuple(d[i] * ahead[i] + value for i in range(GROUP))
            back = tuple(d[i] * back[i] + late for i in range(GROUP))
            out = tree_sum(w[i] * ahead[i] for i in range(GROUP))
            out_grad = tree_sum(w[i] * back[i] for i in range(GROUP))
            if first:
                out = out + c_out[here, :]
                out_grad = out_grad + c_grad[there, :]
            c_out[here, :] = out
            c_grad[there, :] = out_grad
            return ahead, back

        lax.fori_loop(0, ROWS, local_step, ((zero,) * GROUP,) * 2, unroll=4)

    mine = pl.ds(2 * a, 2)
    d2, block_decay, plane_decay = d_tab[mine], block_decay_tab[mine], plane_decay_tab[mine]
    for copy in a_copies:
        copy.wait_recv()

    def over_repeats(value):
        rows_tmp[...] = value
        return [tree_sum(rows_tmp[i, 2 * r : 2 * r + 2, :] for r in range(4)) for i in range(2)]

    cross = jnp.zeros((2, SUB, ROWS), F32)
    for yy in range(NY):
        run = jnp.zeros((2, SUB, ROWS), F32)
        for xx in range(NX):
            slot = yy * NX + xx
            cross = cross + d2 * a_recv[slot, 2:4] * run
            run = block_decay * run + a_recv[slot, 0:2]
        b_send[2 * yy : 2 * yy + 2] = run
        run = jnp.zeros((2, SUB, ROWS), F32)
        for xx in reversed(range(NX)):
            run = block_decay * run + a_recv[yy * NX + xx, 2:4]
        b_send[4 + 2 * yy : 6 + 2 * yy] = run
    b_send[8] = tree_sum(a_recv[slot, 4] for slot in range(PLANE))
    for i, rows in enumerate(over_repeats(cross)):
        b_send[8, 2 * i : 2 * i + 2, :] = b_send[8, 2 * i : 2 * i + 2, :] + rows

    def to_home(zz):
        return remote(b_send, b_recv.at[zz], b_send_sem, b_recv_sem.at[zz], z_id(HOME))

    def answer(zz):
        return remote(owner_out.at[zz], c_recv, c_send_sem.at[zz], c_recv_sem, z_id(zz))

    def result(zz, k):
        return remote(
            r_send, r_recv.at[ch], r_send_sem.at[zz * NCH + k], r_recv_sem.at[k], z_id(zz, k)
        )

    @pl.when(jnp.logical_not(is_home))
    def _():
        to_home(z).start()

    @pl.when(is_home)
    def _():
        b_recv[HOME] = b_send[...]
        for zz in range(NZ):
            if zz != HOME:
                to_home(zz).wait_recv()
        run = jnp.zeros((2, SUB, ROWS), F32)
        cross = jnp.zeros((2, SUB, ROWS), F32)
        for yy in range(NY):
            for zz in range(NZ):
                owner_out[zz, 2 * yy : 2 * yy + 2] = run
                cross = cross + d2 * b_recv[zz, 4 + 2 * yy : 6 + 2 * yy] * run
                run = plane_decay * run + b_recv[zz, 2 * yy : 2 * yy + 2]
        run = jnp.zeros((2, SUB, ROWS), F32)
        for yy in reversed(range(NY)):
            for zz in reversed(range(NZ)):
                owner_out[zz, 4 + 2 * yy : 6 + 2 * yy] = run
                run = plane_decay * run + b_recv[zz, 4 + 2 * yy : 6 + 2 * yy]
        for zz in ANSWER_FIRST:
            answer(zz).start()
        within = tree_sum(b_recv[zz, 8] for zz in range(NZ))
        for i, rows in enumerate(over_repeats(cross)):
            r_send[i] = rows + within[2 * i : 2 * i + 2, :]
        for k in range(1, NCH):
            result(HOME, k).start()
        r_recv[ch] = r_send[...]
        c_recv[...] = owner_out[HOME]

    @pl.when(jnp.logical_not(is_home))
    def _():
        answer(z).wait_recv()

    for yy in range(NY):
        run = c_recv[2 * yy : 2 * yy + 2]
        for xx in range(NX):
            slot = yy * NX + xx
            e_send[slot, 0:2] = run
            run = block_decay * run + a_recv[slot, 0:2]
        run = c_recv[4 + 2 * yy : 6 + 2 * yy]
        for xx in reversed(range(NX)):
            slot = yy * NX + xx
            e_send[slot, 2:4] = run
            run = block_decay * run + a_recv[slot, 2:4]
    e_copies = [
        remote(e_send.at[p], e_recv.at[a], e_send_sem.at[i], e_recv_sem.at[i], device)
        for i, (p, device) in enumerate(zip(plane, plane_ids))
    ]
    for copy in e_copies:
        copy.start()
    e_recv[a] = e_send[a]

    @pl.when(is_home)
    def _():
        for zz in ANSWER_FIRST:
            for k in range(NCH):
                result(zz, k).start()
        for zz in ANSWER_LATER:
            answer(zz).start()
            for k in range(NCH):
                result(zz, k).start()

    pl.when(jnp.logical_not(is_home))(result(z, 0).wait_recv)
    for k in range(1, NCH):
        result(z, k).wait_recv()
    f_send[...] = (r_recv[0] + r_recv[1]) + (r_recv[2] + r_recv[3])
    f_copies = [
        remote(f_send, f_recv.at[a], f_send_sem.at[i], f_recv_sem.at[i], device)
        for i, device in enumerate(plane_ids)
    ]
    for copy in f_copies:
        copy.start()
    f_recv[a] = f_send[...]

    for slots, copies in (
        ([a] + plane[len(FAR) :], e_copies[len(FAR) :]),
        (plane[: len(FAR)], e_copies[: len(FAR)]),
    ):
        for copy in copies:
            copy.wait_recv()
        pairs = [(slot, i) for slot in slots for i in range(2)]
        d = [d_tab[2 * slot + i] for slot, i in pairs]
        w = [w_tab[2 * slot + i] for slot, i in pairs]
        ahead = tuple(w[n] * e_recv[slot, i] for n, (slot, i) in enumerate(pairs))
        back = tuple(w[n] * e_recv[slot, 2 + i] for n, (slot, i) in enumerate(pairs))

        def carry_step(t, carry, d=d):
            ahead, back = carry
            here, there = at(t), at(ROWS - 1 - t)
            ahead = tuple(d[n] * ahead[n] for n in range(GROUP))
            back = tuple(d[n] * back[n] for n in range(GROUP))
            c_out[here, :] = c_out[here, :] + tree_sum(ahead)
            c_grad[there, :] = c_grad[there, :] + tree_sum(back)
            return ahead, back

        lax.fori_loop(0, ROWS, carry_step, (ahead, back), unroll=4)

    stores = []
    for j in range(SUB):
        rows = pl.ds(j * ROWS, ROWS)
        lanes = pl.ds(j, ROWS, stride=SUB)
        gq_out[rows, :] = (g_in[rows, :].astype(F32) * c_out[lanes, :].T).astype(jnp.bfloat16)
        conv_grad = c_grad[lanes, :].T
        gk_out[rows, :] = (conv_grad * v_in[rows, :].astype(F32)).astype(jnp.bfloat16)
        gv_out[rows, :] = (conv_grad * k_in[rows, :].astype(F32)).astype(jnp.bfloat16)
        if j % 2 == 1:
            rows = pl.ds((j - 1) * ROWS, 2 * ROWS)
            for src, dst in ((gq_out, gq_hbm), (gk_out, gk_hbm), (gv_out, gv_hbm)):
                store = pltpu.make_async_copy(
                    src.at[rows, :], dst.at[rows, :], out_sem.at[len(stores)]
                )
                store.start()
                stores.append(store)

    for copy in f_copies:
        copy.wait_recv()
    for m in range(MODES):
        for half in range(2):
            cols = slice(half * ROWS, (half + 1) * ROWS)
            res_out[m : m + 1, cols] = f_recv[m // 2, m % 2, half : half + 1, :]
    res_out[...] = res_out[...] * (jnp.sqrt(2.0 * rate_in[...]) * norm)

    for copy in a_copies + e_copies + f_copies:
        copy.wait_send()
    @pl.when(jnp.logical_not(is_home))
    def _():
        to_home(z).wait_send()

    @pl.when(is_home)
    def _():
        @pl.loop(0, NZ)
        def _(zz):
            pl.when(zz != HOME)(lambda: answer(zz).wait_send())
            pl.when(zz != HOME)(lambda: result(zz, 0).wait_send())
            for k in range(1, NCH):
                result(zz, k).wait_send()

    for store in stores:
        store.wait()


def scan_call(norm, q, k, v, g, rates, residue):
    hbm = pl.BlockSpec(memory_space=pltpu.HBM)
    vmem = pl.BlockSpec(memory_space=pltpu.VMEM)
    big = pltpu.VMEM((CHN, ROWS), F32)
    half = pltpu.VMEM((CHN, ROWS), jnp.bfloat16)
    table = pltpu.VMEM((MODES, SUB, ROWS), F32)
    small = pltpu.VMEM((MODES, FG), F32)
    dma = pltpu.SemaphoreType.DMA
    wide = jax.ShapeDtypeStruct((CHN, ROWS), jnp.bfloat16)
    return pl.pallas_call(
        functools.partial(scan_kernel, norm),
        out_shape=(wide, wide, wide, jax.ShapeDtypeStruct((MODES, FG), F32)),
        in_specs=[hbm] * 6,
        out_specs=(hbm, hbm, hbm, vmem),
        scratch_shapes=[
            half, half, half, half, small, small,
            big, big, big, big, half, half, half,
            table, table, table, table,
            pltpu.VMEM((PLANE, 5, SUB, ROWS), F32),
            pltpu.VMEM((PLANE, 5, SUB, ROWS), F32),
            pltpu.VMEM((2, SUB, ROWS), F32),
            pltpu.VMEM((9, SUB, ROWS), F32),
            pltpu.VMEM((NZ, 9, SUB, ROWS), F32),
            pltpu.VMEM((NZ, 8, SUB, ROWS), F32),
            pltpu.VMEM((8, SUB, ROWS), F32),
            pltpu.VMEM((2, 2, ROWS), F32),
            pltpu.VMEM((NCH, 2, 2, ROWS), F32),
            pltpu.VMEM((PLANE, 4, SUB, ROWS), F32),
            pltpu.VMEM((PLANE, 4, SUB, ROWS), F32),
            pltpu.VMEM((2, 2, ROWS), F32),
            pltpu.VMEM((PLANE, 2, 2, ROWS), F32),
            dma((6,)), dma((12,)),
            dma((PLANE - 1,)), dma((PLANE - 1,)), dma, dma((NZ,)), dma((NZ,)), dma,
            dma((NZ * NCH,)), dma((NCH,)),
            dma((PLANE - 1,)), dma((PLANE - 1,)), dma((PLANE - 1,)), dma((PLANE - 1,)),
        ],
        compiler_params=pltpu.CompilerParams(
            collective_id=0, has_side_effects=True, vmem_limit_bytes=63 * 2**20
        ),
        name="scan_states",
    )(q, k, v, g, rates, residue)


def finish_kernel(*refs):
    half = (len(refs) - 2) // 3
    srcs, dsts, held = refs[:half], refs[half : 2 * half], refs[2 * half : 3 * half]
    in_sem, out_sem = refs[3 * half :]
    loads = [pltpu.make_async_copy(srcs[i], held[i], in_sem.at[i]) for i in range(half)]
    stores = [pltpu.make_async_copy(held[i], dsts[i], out_sem.at[i]) for i in range(half)]
    for load in loads:
        load.start()
    for load, store in zip(loads, stores):
        load.wait()
        store.start()
    for store in stores:
        store.wait()


def finish_call(*results):
    n = len(results)
    hbm = pl.BlockSpec(memory_space=pl.ANY)
    return pl.pallas_call(
        finish_kernel,
        out_shape=tuple(jax.ShapeDtypeStruct(r.shape, r.dtype) for r in results),
        in_specs=[hbm] * n,
        out_specs=(hbm,) * n,
        scratch_shapes=[pltpu.VMEM(r.shape, r.dtype) for r in results]
        + [pltpu.SemaphoreType.DMA((n,)), pltpu.SemaphoreType.DMA((n,))],
        name="finish",
    )(*results)


def local(q_branch, k_branch, v_branch, grad_gated, decay_rates, residue):
    norm = 1.0 / math.sqrt(q_branch.shape[1] * lax.axis_size("ctx"))
    grad_q, grad_k, grad_v, res = finish_call(
        *scan_call(norm, q_branch, k_branch, v_branch, grad_gated, decay_rates.T, residue.T)
    )
    return grad_q, grad_k, grad_v, res.T


def solution(mesh):
    in_specs = (P("ch", "ctx"), P("ch", "ctx"), P("ch", "ctx"), P("ch", "ctx"), P(), P())
    out_specs = (P("ch", "ctx"), P("ch", "ctx"), P("ch", "ctx"), P())
    return jax.shard_map(local, mesh=mesh, in_specs=in_specs, out_specs=out_specs, check_vma=False)
```

time: 44.2 us -> 40.1 us (0.907)
  the two profiles are of different devices: /device:TPU:1 before, /device:TPU:32 now
where the time goes in v2:
time: 40.1 us; the launch traced here: 39.9 us
  Pallas kernels  39.3 us (98%)
  between operations  0.64 us (2%)
    pallas_call x1, Pallas kernels, scan_call(): pl.pallas_call(functools.partial(scan_kernel, norm), out_shape=(wide, wid...  37.4 us
    pallas_call x1, Pallas kernels, finish_call(): pl.pallas_call(finish_kernel, out_shape=tuple((jax.ShapeDtypeStruct(r.sha...  1.9 us

profile of v2, /device:TPU:32, one launch (start us, length us, event | category | flops | bytes accessed | tf_op | source)
XLA Modules:
  0.0 39.9 jit_solution(11405852903378276935)
XLA Ops:
  0.6 37.4 %scan_states.1 = (bf16[1024,128]{1,0:T(8,128)(2,1)}, bf16[1024,128]{1,0:T(8,128)(2,1)}, bf16[1024,128]{1,0:T(8,128)(2,1)}, f32[16,256]{1,0:T(8,128)}) custom-call(bf16[1024,128]{1,0:T(8,128)(2,1)} %q_hbm.1, bf16[1024,128]{1,0:T(8,128)(2,1)} %k_hbm.1, bf16[1024,128]{1,0:T(8,128)(2,1)} %v_hbm.1, bf16[1024,128]{1,0:T(8,128)(2,1)} %g_hbm.1, f32[16,256]{1,0:T(8,128)} %bitcast.3, ...), custom_call_target="tpu_custom_call" | custom-call | tf_op jit(solution)/shard_map/scan_states/pallas_call | solution.py:384
  38.0 1.9 %finish.1 = (bf16[1024,128]{1,0:T(8,128)(2,1)}, bf16[1024,128]{1,0:T(8,128)(2,1)}, bf16[1024,128]{1,0:T(8,128)(2,1)}, f32[16,256]{1,0:T(8,128)}) custom-call(bf16[1024,128]{1,0:T(8,128)(2,1)} %get-tuple-element.12.refs_0_, bf16[1024,128]{1,0:T(8,128)(2,1)} %get-tuple-element.13.refs_1_, bf16[1024,128]{1,0:T(8,128)(2,1)} %get-tuple-element.14.refs_2_, ...), custom_call_target="tpu_custom_call" | custom-call | tf_op jit(solution)/shard_map/finish/pallas_call | solution.py:436

commit v3 on v2

--- a/solution.py
+++ b/solution.py
@@ -24,6 +24,7 @@
 ANSWER_LATER = (4, 5, 6, 7, 15, 8, 14, 9, 13, 10, 12, 11)
 NEAR = ((0, 1), (0, 3), (1, 0))
 FAR = ((1, 2), (1, 1), (1, 3), (0, 2))
+PARTS = ((4, 5, 6), (1, 2, 3), (0,))
 
 
 def tree_sum(terms):
@@ -38,15 +39,15 @@
 
 def scan_kernel(
     norm,
-    q_hbm, k_hbm, v_hbm, g_hbm, rate_hbm, resid_hbm,
-    gq_hbm, gk_hbm, gv_hbm, res_out,
-    q_in, k_in, v_in, g_in, rate_in, resid_in,
-    x_kv, x_g, c_out, c_grad, gq_out, gk_out, gv_out,
+    q_hbm, k_hbm, v_hbm, g_hbm, poles_hbm,
+    gq_out, gk_out, gv_out, res_out,
+    q_in, k_in, v_in, g_in, poles_in,
+    x_kv, x_g, c_out, c_grad,
     d_tab, w_tab, plane_decay_tab, block_decay_tab,
-    a_send, a_recv, rows_tmp, b_send, b_recv, owner_out, c_recv, r_send, r_recv, e_send, e_recv,
-    f_send, f_recv, in_sem, out_sem,
+    a_send, a_recv, rows_tmp, b_send, b_recv, owner_out, c_recv, r_send, r_recv, r_sum, e_send, e_recv,
+    f_recv, in_sem,
     a_send_sem, a_recv_sem, b_send_sem, b_recv_sem, c_send_sem, c_recv_sem,
-    r_send_sem, r_recv_sem, e_send_sem, e_recv_sem, f_send_sem, f_recv_sem,
+    r_send_sem, r_recv_sem, g_send_sem, g_recv_sem, e_send_sem, e_recv_sem, f_send_sem, f_recv_sem,
 ):
     ctx, ch = lax.axis_index("ctx"), lax.axis_index("ch")
     y, z, x = lax.div(ctx, NX * NZ), lax.rem(lax.div(ctx, NX), NZ), lax.rem(ctx, NX)
@@ -60,19 +61,26 @@
     plane = [y_plus[dy] * NX + x_plus[dx] for dy, dx in FAR + NEAR]
     plane_ids = [((y_plus[dy] * NZ + z) * NX + x_plus[dx], ch) for dy, dx in FAR + NEAR]
 
-    def z_id(zz, dch=0):
-        return column + zz * NX, ch_plus[dch]
+    line_ids = [(plane_ids[i], plane[i]) for i, (dy, dx) in enumerate(FAR + NEAR) if dy == 0]
+
+    def z_id(zz):
+        return column + zz * NX, ch
+
+    def cross_id(k, dy):
+        return (y_plus[dy] * NZ + HOME) * NX + x, ch_plus[k]
+
+    cross = [(k, dy) for k in range(NCH) for dy in reversed(range(NY)) if k or dy]
 
     loads = [
         pltpu.make_async_copy(src, dst, in_sem.at[i])
         for i, (src, dst) in enumerate(
             [
                 (k_hbm, k_in), (v_hbm, v_in), (g_hbm, g_in), (q_hbm, q_in),
-                (rate_hbm, rate_in), (resid_hbm, resid_in),
+                (poles_hbm, poles_in),
             ]
         )
     ]
-    for i in (4, 5, 0, 1, 2, 3):
+    for i in (4, 0, 1, 2, 3):
         loads[i].start()
 
     barrier = pltpu.get_barrier_semaphore()
@@ -85,25 +93,21 @@
 
     @pl.when(jnp.logical_not(is_home))
     def _():
-        for k in range(NCH):
-            greet(z_id(HOME, k))
+        greet(z_id(HOME))
 
     @pl.when(is_home)
     def _():
-        for k in range(1, NCH):
-            greet(z_id(HOME, k))
-
-        @pl.loop(0, NZ)
+        for k, dy in cross:
+            if k != 0:
+                greet(cross_id(k, dy))
+
+        @pl.loop(1, NZ)
         def _(zz):
-            @pl.when(zz != HOME)
-            def _():
-                for k in range(NCH):
-                    greet(z_id(zz, k))
+            greet(z_id(zz))
 
     loads[4].wait()
-    loads[5].wait()
-    rate_t = rate_in[...]
-    weight_t = resid_in[...] * jnp.sqrt(2.0 * rate_t)
+    rate_t = poles_in[0]
+    weight_t = poles_in[1] * jnp.sqrt(2.0 * rate_t)
     odd = lax.broadcasted_iota(jnp.int32, (SUB, ROWS), 0) % 2 == 1
     for m in range(MODES):
         rate = jnp.where(odd, rate_t[m : m + 1, ROWS:], rate_t[m : m + 1, :ROWS])
@@ -154,7 +158,8 @@
                 acc[i][2 * r : 2 * r + 2, :] for r in range(4)
             )
 
-    pl.semaphore_wait(barrier, len(plane) + jnp.where(is_home, NZ * NCH - 1, NCH))
+    beyond = jnp.where(is_home, (NCH - 1) * NY + NZ - 1, 1)
+    pl.semaphore_wait(barrier, len(plane) + beyond)
 
     def remote(src, dst, send_sem, recv_sem, device):
         return pltpu.make_async_remote_copy(
@@ -201,12 +206,12 @@
         rows_tmp[...] = value
         return [tree_sum(rows_tmp[i, 2 * r : 2 * r + 2, :] for r in range(4)) for i in range(2)]
 
-    cross = jnp.zeros((2, SUB, ROWS), F32)
+    between = jnp.zeros((2, SUB, ROWS), F32)
     for yy in range(NY):
         run = jnp.zeros((2, SUB, ROWS), F32)
         for xx in range(NX):
             slot = yy * NX + xx
-            cross = cross + d2 * a_recv[slot, 2:4] * run
+            between = between + d2 * a_recv[slot, 2:4] * run
             run = block_decay * run + a_recv[slot, 0:2]
         b_send[2 * yy : 2 * yy + 2] = run
         run = jnp.zeros((2, SUB, ROWS), F32)
@@ -214,7 +219,7 @@
             run = block_decay * run + a_recv[yy * NX + xx, 2:4]
         b_send[4 + 2 * yy : 6 + 2 * yy] = run
     b_send[8] = tree_sum(a_recv[slot, 4] for slot in range(PLANE))
-    for i, rows in enumerate(over_repeats(cross)):
+    for i, rows in enumerate(over_repeats(between)):
         b_send[8, 2 * i : 2 * i + 2, :] = b_send[8, 2 * i : 2 * i + 2, :] + rows
 
     def to_home(zz):
@@ -223,10 +228,13 @@
     def answer(zz):
         return remote(owner_out.at[zz], c_recv, c_send_sem.at[zz], c_recv_sem, z_id(zz))
 
-    def result(zz, k):
+    def result(k, dy):
         return remote(
-            r_send, r_recv.at[ch], r_send_sem.at[zz * NCH + k], r_recv_sem.at[k], z_id(zz, k)
+            r_send, r_recv.at[ch, y], r_send_sem.at[k, dy], r_recv_sem.at[k, dy], cross_id(k, dy)
         )
+
+    def summed(zz):
+        return remote(r_sum, r_sum, g_send_sem.at[zz], g_recv_sem, z_id(zz))
 
     @pl.when(jnp.logical_not(is_home))
     def _():
@@ -239,12 +247,17 @@
             if zz != HOME:
                 to_home(zz).wait_recv()
         run = jnp.zeros((2, SUB, ROWS), F32)
-        cross = jnp.zeros((2, SUB, ROWS), F32)
+        between = jnp.zeros((2, SUB, ROWS), F32)
         for yy in range(NY):
             for zz in range(NZ):
                 owner_out[zz, 2 * yy : 2 * yy + 2] = run
-                cross = cross + d2 * b_recv[zz, 4 + 2 * yy : 6 + 2 * yy] * run
+                between = between + d2 * b_recv[zz, 4 + 2 * yy : 6 + 2 * yy] * run
                 run = plane_decay * run + b_recv[zz, 2 * yy : 2 * yy + 2]
+        within = tree_sum(b_recv[zz, 8] for zz in range(NZ))
+        for i, rows in enumerate(over_repeats(between)):
+            r_send[i] = rows + within[2 * i : 2 * i + 2, :]
+        for k, dy in cross:
+            result(k, dy).start()
         run = jnp.zeros((2, SUB, ROWS), F32)
         for yy in reversed(range(NY)):
             for zz in reversed(range(NZ)):
@@ -252,12 +265,7 @@
                 run = plane_decay * run + b_recv[zz, 4 + 2 * yy : 6 + 2 * yy]
         for zz in ANSWER_FIRST:
             answer(zz).start()
-        within = tree_sum(b_recv[zz, 8] for zz in range(NZ))
-        for i, rows in enumerate(over_repeats(cross)):
-            r_send[i] = rows + within[2 * i : 2 * i + 2, :]
-        for k in range(1, NCH):
-            result(HOME, k).start()
-        r_recv[ch] = r_send[...]
+        r_recv[ch, y] = r_send[...]
         c_recv[...] = owner_out[HOME]
 
     @pl.when(jnp.logical_not(is_home))
@@ -285,32 +293,30 @@
 
     @pl.when(is_home)
     def _():
-        for zz in ANSWER_FIRST:
-            for k in range(NCH):
-                result(zz, k).start()
         for zz in ANSWER_LATER:
             answer(zz).start()
-            for k in range(NCH):
-                result(zz, k).start()
-
-    pl.when(jnp.logical_not(is_home))(result(z, 0).wait_recv)
-    for k in range(1, NCH):
-        result(z, k).wait_recv()
-    f_send[...] = (r_recv[0] + r_recv[1]) + (r_recv[2] + r_recv[3])
+
+    @pl.when(is_home)
+    def _():
+        for k, dy in cross:
+            result(k, dy).wait_recv()
+        r_sum[...] = (r_recv[0] + r_recv[1]) + (r_recv[2] + r_recv[3])
+        for zz in ANSWER_FIRST + ANSWER_LATER:
+            summed(zz).start()
+
+    pl.when(jnp.logical_not(is_home))(summed(z).wait_recv)
     f_copies = [
-        remote(f_send, f_recv.at[a], f_send_sem.at[i], f_recv_sem.at[i], device)
-        for i, device in enumerate(plane_ids)
+        remote(r_sum, f_recv.at[x], f_send_sem.at[i], f_recv_sem.at[i], device)
+        for i, (device, _) in enumerate(line_ids)
     ]
     for copy in f_copies:
         copy.start()
-    f_recv[a] = f_send[...]
-
-    for slots, copies in (
-        ([a] + plane[len(FAR) :], e_copies[len(FAR) :]),
-        (plane[: len(FAR)], e_copies[: len(FAR)]),
-    ):
-        for copy in copies:
-            copy.wait_recv()
+    f_recv[x] = r_sum[...]
+
+    for members in PARTS:
+        for n in members:
+            e_copies[n].wait_recv()
+        slots = [plane[n] for n in members] + ([a] if members == PARTS[0] else [])
         pairs = [(slot, i) for slot in slots for i in range(2)]
         d = [d_tab[2 * slot + i] for slot, i in pairs]
         w = [w_tab[2 * slot + i] for slot, i in pairs]
@@ -320,15 +326,14 @@
         def carry_step(t, carry, d=d):
             ahead, back = carry
             here, there = at(t), at(ROWS - 1 - t)
-            ahead = tuple(d[n] * ahead[n] for n in range(GROUP))
-            back = tuple(d[n] * back[n] for n in range(GROUP))
+            ahead = tuple(d[n] * ahead[n] for n in range(len(d)))
+            back = tuple(d[n] * back[n] for n in range(len(d)))
             c_out[here, :] = c_out[here, :] + tree_sum(ahead)
             c_grad[there, :] = c_grad[there, :] + tree_sum(back)
             return ahead, back
 
         lax.fori_loop(0, ROWS, carry_step, (ahead, back), unroll=4)
 
-    stores = []
     for j in range(SUB):
         rows = pl.ds(j * ROWS, ROWS)
         lanes = pl.ds(j, ROWS, stride=SUB)
@@ -336,23 +341,14 @@
         conv_grad = c_grad[lanes, :].T
         gk_out[rows, :] = (conv_grad * v_in[rows, :].astype(F32)).astype(jnp.bfloat16)
         gv_out[rows, :] = (conv_grad * k_in[rows, :].astype(F32)).astype(jnp.bfloat16)
-        if j % 2 == 1:
-            rows = pl.ds((j - 1) * ROWS, 2 * ROWS)
-            for src, dst in ((gq_out, gq_hbm), (gk_out, gk_hbm), (gv_out, gv_hbm)):
-                store = pltpu.make_async_copy(
-                    src.at[rows, :], dst.at[rows, :], out_sem.at[len(stores)]
-                )
-                store.start()
-                stores.append(store)
 
     for copy in f_copies:
         copy.wait_recv()
     for m in range(MODES):
         for half in range(2):
             cols = slice(half * ROWS, (half + 1) * ROWS)
-            res_out[m : m + 1, cols] = f_recv[m // 2, m % 2, half : half + 1, :]
-    res_out[...] = res_out[...] * (jnp.sqrt(2.0 * rate_in[...]) * norm)
-
+            res_out[m : m + 1, cols] = f_recv[m // 2 % NX, m // 2 // NX, m % 2, half : half + 1, :]
+    res_out[...] = res_out[...] * (jnp.sqrt(2.0 * poles_in[0]) * norm)
     for copy in a_copies + e_copies + f_copies:
         copy.wait_send()
     @pl.when(jnp.logical_not(is_home))
@@ -361,34 +357,33 @@
 
     @pl.when(is_home)
     def _():
-        @pl.loop(0, NZ)
+        @pl.loop(1, NZ)
         def _(zz):
-            pl.when(zz != HOME)(lambda: answer(zz).wait_send())
-            pl.when(zz != HOME)(lambda: result(zz, 0).wait_send())
-            for k in range(1, NCH):
-                result(zz, k).wait_send()
-
-    for store in stores:
-        store.wait()
-
-
-def scan_call(norm, q, k, v, g, rates, residue):
+            answer(zz).wait_send()
+
+        for k, dy in cross:
+            result(k, dy).wait_send()
+
+        @pl.loop(1, NZ)
+        def _(zz):
+            summed(zz).wait_send()
+
+
+def scan_call(norm, q, k, v, g, poles):
     hbm = pl.BlockSpec(memory_space=pltpu.HBM)
-    vmem = pl.BlockSpec(memory_space=pltpu.VMEM)
     big = pltpu.VMEM((CHN, ROWS), F32)
     half = pltpu.VMEM((CHN, ROWS), jnp.bfloat16)
     table = pltpu.VMEM((MODES, SUB, ROWS), F32)
-    small = pltpu.VMEM((MODES, FG), F32)
     dma = pltpu.SemaphoreType.DMA
     wide = jax.ShapeDtypeStruct((CHN, ROWS), jnp.bfloat16)
     return pl.pallas_call(
         functools.partial(scan_kernel, norm),
         out_shape=(wide, wide, wide, jax.ShapeDtypeStruct((MODES, FG), F32)),
-        in_specs=[hbm] * 6,
-        out_specs=(hbm, hbm, hbm, vmem),
+        in_specs=[hbm] * 5,
+        out_specs=(pl.BlockSpec(memory_space=pltpu.VMEM),) * 4,
         scratch_shapes=[
-            half, half, half, half, small, small,
-            big, big, big, big, half, half, half,
+            half, half, half, half, pltpu.VMEM((2, MODES, FG), F32),
+            big, big, big, big,
             table, table, table, table,
             pltpu.VMEM((PLANE, 5, SUB, ROWS), F32),
             pltpu.VMEM((PLANE, 5, SUB, ROWS), F32),
@@ -398,56 +393,52 @@
             pltpu.VMEM((NZ, 8, SUB, ROWS), F32),
             pltpu.VMEM((8, SUB, ROWS), F32),
             pltpu.VMEM((2, 2, ROWS), F32),
-            pltpu.VMEM((NCH, 2, 2, ROWS), F32),
+            pltpu.VMEM((NCH, NY, 2, 2, ROWS), F32),
+            pltpu.VMEM((NY, 2, 2, ROWS), F32),
             pltpu.VMEM((PLANE, 4, SUB, ROWS), F32),
             pltpu.VMEM((PLANE, 4, SUB, ROWS), F32),
-            pltpu.VMEM((2, 2, ROWS), F32),
-            pltpu.VMEM((PLANE, 2, 2, ROWS), F32),
-            dma((6,)), dma((12,)),
+            pltpu.VMEM((NX, NY, 2, 2, ROWS), F32),
+            dma((5,)),
             dma((PLANE - 1,)), dma((PLANE - 1,)), dma, dma((NZ,)), dma((NZ,)), dma,
-            dma((NZ * NCH,)), dma((NCH,)),
-            dma((PLANE - 1,)), dma((PLANE - 1,)), dma((PLANE - 1,)), dma((PLANE - 1,)),
+            dma((NCH, NY)), dma((NCH, NY)), dma((NZ,)), dma,
+            dma((PLANE - 1,)), dma((PLANE - 1,)), dma((NX - 1,)), dma((NX - 1,)),
         ],
         compiler_params=pltpu.CompilerParams(
-            collective_id=0, has_side_effects=True, vmem_limit_bytes=63 * 2**20
+            collective_id=0, has_side_effects=True, vmem_limit_bytes=54336 * 2**10
         ),
         name="scan_states",
-    )(q, k, v, g, rates, residue)
+    )(q, k, v, g, poles)
 
 
 def finish_kernel(*refs):
-    half = (len(refs) - 2) // 3
-    srcs, dsts, held = refs[:half], refs[half : 2 * half], refs[2 * half : 3 * half]
-    in_sem, out_sem = refs[3 * half :]
-    loads = [pltpu.make_async_copy(srcs[i], held[i], in_sem.at[i]) for i in range(half)]
-    stores = [pltpu.make_async_copy(held[i], dsts[i], out_sem.at[i]) for i in range(half)]
-    for load in loads:
-        load.start()
-    for load, store in zip(loads, stores):
-        load.wait()
-        store.start()
-    for store in stores:
-        store.wait()
+    half = len(refs) // 2
+    srcs, dsts, sems = refs[:half], refs[half : 2 * half], refs[2 * half]
+    copies = [pltpu.make_async_copy(srcs[i], dsts[i], sems.at[i]) for i in range(half)]
+    for copy in copies:
+        copy.start()
+    for copy in copies:
+        copy.wait()
 
 
 def finish_call(*results):
     n = len(results)
-    hbm = pl.BlockSpec(memory_space=pl.ANY)
+    anywhere = pl.BlockSpec(memory_space=pl.ANY)
     return pl.pallas_call(
         finish_kernel,
         out_shape=tuple(jax.ShapeDtypeStruct(r.shape, r.dtype) for r in results),
-        in_specs=[hbm] * n,
-        out_specs=(hbm,) * n,
-        scratch_shapes=[pltpu.VMEM(r.shape, r.dtype) for r in results]
-        + [pltpu.SemaphoreType.DMA((n,)), pltpu.SemaphoreType.DMA((n,))],
+        in_specs=[anywhere] * n,
+        out_specs=(anywhere,) * n,
+        scratch_shapes=[pltpu.SemaphoreType.DMA((n,))],
+        compiler_params=pltpu.CompilerParams(vmem_limit_bytes=4 * 2**20),
         name="finish",
     )(*results)
 
 
 def local(q_branch, k_branch, v_branch, grad_gated, decay_rates, residue):
     norm = 1.0 / math.sqrt(q_branch.shape[1] * lax.axis_size("ctx"))
+    poles = jnp.stack([decay_rates.T, residue.T])
     grad_q, grad_k, grad_v, res = finish_call(
-        *scan_call(norm, q_branch, k_branch, v_branch, grad_gated, decay_rates.T, residue.T)
+        *scan_call(norm, q_branch, k_branch, v_branch, grad_gated, poles)
     )
     return grad_q, grad_k, grad_v, res.T
 

time: 40.1 us -> 39 us (0.973)
  Pallas kernels: 39.3 us -> 37.3 us
  other arithmetic: 0 us -> 0.74 us
    pallas_call x1, Pallas kernels: 37.4 us -> 36.4 us  [scan_call(): pl.pallas_call(functools.partial(scan_kernel, norm), out_shape=(wide, wid...]
    pallas_call x1, Pallas kernels: 1.9 us -> 0.91 us  [finish_call(): pl.pallas_call(finish_kernel, out_shape=tuple((jax.ShapeDtypeStruct(r.sha...]
    another operation x0 -> x1, other arithmetic: none -> 0.74 us  [local(): poles = jnp.stack([decay_rates.T, residue.T])]
where the time goes in v3:
time: 39 us; the launch traced here: 38.7 us
  Pallas kernels  37.3 us (96%)
  other arithmetic  0.74 us (2%)
  between operations  0.64 us (2%)
    pallas_call x1, Pallas kernels, scan_call(): pl.pallas_call(functools.partial(scan_kernel, norm), out_shape=(wide, wid...  36.4 us
    pallas_call x1, Pallas kernels, finish_call(): pl.pallas_call(finish_kernel, out_shape=tuple((jax.ShapeDtypeStruct(r.sha...  0.91 us

profile of v3, /device:TPU:32, one launch (start us, length us, event | category | flops | bytes accessed | tf_op | source)
XLA Modules:
  0.0 38.7 jit_solution(8254151771876606466)
XLA Ops:
  0.6 0.7 %pad_maximum_fusion.poles_hbm = f32[2,16,256]{2,1,0:T(8,128)S(1)} fusion(f32[1,16,256]{2,1,0:T(8,128)} %bitcast.7, f32[1,16,256]{2,1,0:T(8,128)} %bitcast.8), kind=kLoop, calls=%fused_computation | loop fusion | flops 8192 | bytes 65536 | tf_op jit(solution)/shard_map/stack | solution.py:439
  1.4 36.4 %scan_states.1 = (bf16[1024,128]{1,0:T(8,128)(2,1)S(1)}, bf16[1024,128]{1,0:T(8,128)(2,1)S(1)}, bf16[1024,128]{1,0:T(8,128)(2,1)S(1)}, f32[16,256]{1,0:T(8,128)S(1)}) custom-call(bf16[1024,128]{1,0:T(8,128)(2,1)} %q_hbm.1, bf16[1024,128]{1,0:T(8,128)(2,1)} %k_hbm.1, bf16[1024,128]{1,0:T(8,128)(2,1)} %v_hbm.1, bf16[1024,128]{1,0:T(8,128)(2,1)} %g_hbm.1, ...), custom_call_target="tpu_custom_call" | custom-call | tf_op jit(solution)/shard_map/scan_states/pallas_call | solution.py:379
  37.8 0.9 %finish.1 = (bf16[1024,128]{1,0:T(8,128)(2,1)}, bf16[1024,128]{1,0:T(8,128)(2,1)}, bf16[1024,128]{1,0:T(8,128)(2,1)}, f32[16,256]{1,0:T(8,128)}) custom-call(bf16[1024,128]{1,0:T(8,128)(2,1)S(1)} %get-tuple-element.12.refs_0_, bf16[1024,128]{1,0:T(8,128)(2,1)S(1)} %get-tuple-element.13.refs_1_, bf16[1024,128]{1,0:T(8,128)(2,1)S(1)} %get-tuple-element.14.refs_2_, ...), custom_call_target="tpu_custom_call" | custom-call | tf_op jit(solution)/shard_map/finish/pallas_call | solution.py:426

commit v4 on v3

--- a/solution.py
+++ b/solution.py
@@ -20,11 +20,12 @@
 SUB = 8
 GROUP = 8
 HOME = 0
-ANSWER_FIRST = (1, 2, 3)
-ANSWER_LATER = (4, 5, 6, 7, 15, 8, 14, 9, 13, 10, 12, 11)
+ANSWER_FIRST = (1, 2, 3, 4, 5, 6, 7, 8)
+ANSWER_LATER = (9, 15, 10, 14, 11, 13, 12)
+DIRECT = 5
+ALONG = (2, 1, 3)
 NEAR = ((0, 1), (0, 3), (1, 0))
 FAR = ((1, 2), (1, 1), (1, 3), (0, 2))
-PARTS = ((4, 5, 6), (1, 2, 3), (0,))
 
 
 def tree_sum(terms):
@@ -53,6 +54,7 @@
     y, z, x = lax.div(ctx, NX * NZ), lax.rem(lax.div(ctx, NX), NZ), lax.rem(ctx, NX)
     a = y * NX + x
     is_home = z == HOME
+    is_direct = z < DIRECT
     x_plus = [lax.rem(x + k, NX) for k in range(NX)]
     y_plus = [lax.rem(y + k, NY) for k in range(NY)]
     ch_plus = [lax.rem(ch + k, NCH) for k in range(NCH)]
@@ -61,7 +63,8 @@
     plane = [y_plus[dy] * NX + x_plus[dx] for dy, dx in FAR + NEAR]
     plane_ids = [((y_plus[dy] * NZ + z) * NX + x_plus[dx], ch) for dy, dx in FAR + NEAR]
 
-    line_ids = [(plane_ids[i], plane[i]) for i, (dy, dx) in enumerate(FAR + NEAR) if dy == 0]
+    def line_id(zz, k):
+        return (y * NZ + zz) * NX + x_plus[k], ch
 
     def z_id(zz):
         return column + zz * NX, ch
@@ -95,6 +98,11 @@
     def _():
         greet(z_id(HOME))
 
+    @pl.when(jnp.logical_and(is_direct, jnp.logical_not(is_home)))
+    def _():
+        for k in ALONG:
+            greet(line_id(HOME, k))
+
     @pl.when(is_home)
     def _():
         for k, dy in cross:
@@ -104,6 +112,11 @@
         @pl.loop(1, NZ)
         def _(zz):
             greet(z_id(zz))
+
+        @pl.loop(1, DIRECT)
+        def _(zz):
+            for k in ALONG:
+                greet(line_id(zz, k))
 
     loads[4].wait()
     rate_t = poles_in[0]
@@ -149,7 +162,7 @@
             return ahead, back, acc
 
         start = ((zero,) * GROUP,) * 3
-        ahead, back, acc = lax.fori_loop(0, ROWS, end_step, start, unroll=4)
+        ahead, back, acc = lax.fori_loop(0, ROWS, end_step, start, unroll=16)
         for i, m in enumerate(modes):
             a_send[m // 2, m % 2] = ahead[i]
             a_send[m // 2, 2 + m % 2] = back[i]
@@ -158,7 +171,8 @@
                 acc[i][2 * r : 2 * r + 2, :] for r in range(4)
             )
 
-    beyond = jnp.where(is_home, (NCH - 1) * NY + NZ - 1, 1)
+    at_home = (NCH - 1) * NY + NZ - 1 + (DIRECT - 1) * len(ALONG)
+    beyond = jnp.where(is_home, at_home, jnp.where(is_direct, NX, 1))
     pl.semaphore_wait(barrier, len(plane) + beyond)
 
     def remote(src, dst, send_sem, recv_sem, device):
@@ -195,7 +209,7 @@
             c_grad[there, :] = out_grad
             return ahead, back
 
-        lax.fori_loop(0, ROWS, local_step, ((zero,) * GROUP,) * 2, unroll=4)
+        lax.fori_loop(0, ROWS, local_step, ((zero,) * GROUP,) * 2, unroll=16)
 
     mine = pl.ds(2 * a, 2)
     d2, block_decay, plane_decay = d_tab[mine], block_decay_tab[mine], plane_decay_tab[mine]
@@ -235,6 +249,16 @@
 
     def summed(zz):
         return remote(r_sum, r_sum, g_send_sem.at[zz], g_recv_sem, z_id(zz))
+
+    def along(zz, k):
+        return remote(
+            r_sum, f_recv.at[x], f_send_sem.at[zz, k], f_recv_sem.at[k], line_id(zz, k)
+        )
+
+    def pass_on():
+        for k in ALONG:
+            along(z, k).start()
+        f_recv[x] = r_sum[...]
 
     @pl.when(jnp.logical_not(is_home))
     def _():
@@ -301,38 +325,36 @@
         for k, dy in cross:
             result(k, dy).wait_recv()
         r_sum[...] = (r_recv[0] + r_recv[1]) + (r_recv[2] + r_recv[3])
+        for zz in range(1, DIRECT):
+            for k in ALONG + (0,):
+                along(zz, k).start()
+        pass_on()
         for zz in ANSWER_FIRST + ANSWER_LATER:
-            summed(zz).start()
-
-    pl.when(jnp.logical_not(is_home))(summed(z).wait_recv)
-    f_copies = [
-        remote(r_sum, f_recv.at[x], f_send_sem.at[i], f_recv_sem.at[i], device)
-        for i, (device, _) in enumerate(line_ids)
-    ]
-    for copy in f_copies:
-        copy.start()
-    f_recv[x] = r_sum[...]
-
-    for members in PARTS:
-        for n in members:
-            e_copies[n].wait_recv()
-        slots = [plane[n] for n in members] + ([a] if members == PARTS[0] else [])
-        pairs = [(slot, i) for slot in slots for i in range(2)]
-        d = [d_tab[2 * slot + i] for slot, i in pairs]
-        w = [w_tab[2 * slot + i] for slot, i in pairs]
-        ahead = tuple(w[n] * e_recv[slot, i] for n, (slot, i) in enumerate(pairs))
-        back = tuple(w[n] * e_recv[slot, 2 + i] for n, (slot, i) in enumerate(pairs))
-
-        def carry_step(t, carry, d=d):
-            ahead, back = carry
-            here, there = at(t), at(ROWS - 1 - t)
-            ahead = tuple(d[n] * ahead[n] for n in range(len(d)))
-            back = tuple(d[n] * back[n] for n in range(len(d)))
-            c_out[here, :] = c_out[here, :] + tree_sum(ahead)
-            c_grad[there, :] = c_grad[there, :] + tree_sum(back)
-            return ahead, back
-
-        lax.fori_loop(0, ROWS, carry_step, (ahead, back), unroll=4)
+            if zz >= DIRECT:
+                summed(zz).start()
+
+    @pl.when(jnp.logical_not(is_direct))
+    def _():
+        summed(z).wait_recv()
+        pass_on()
+
+    for copy in e_copies:
+        copy.wait_recv()
+    d = [d_tab[m] for m in range(MODES)]
+    w = [w_tab[m] for m in range(MODES)]
+    ahead = tuple(w[m] * e_recv[m // 2, m % 2] for m in range(MODES))
+    back = tuple(w[m] * e_recv[m // 2, 2 + m % 2] for m in range(MODES))
+
+    def carry_step(t, carry):
+        ahead, back = carry
+        here, there = at(t), at(ROWS - 1 - t)
+        ahead = tuple(d[n] * ahead[n] for n in range(len(d)))
+        back = tuple(d[n] * back[n] for n in range(len(d)))
+        c_out[here, :] = c_out[here, :] + tree_sum(ahead)
+        c_grad[there, :] = c_grad[there, :] + tree_sum(back)
+        return ahead, back
+
+    lax.fori_loop(0, ROWS, carry_step, (ahead, back), unroll=16)
 
     for j in range(SUB):
         rows = pl.ds(j * ROWS, ROWS)
@@ -342,14 +364,15 @@
         gk_out[rows, :] = (conv_grad * v_in[rows, :].astype(F32)).astype(jnp.bfloat16)
         gv_out[rows, :] = (conv_grad * k_in[rows, :].astype(F32)).astype(jnp.bfloat16)
 
-    for copy in f_copies:
-        copy.wait_recv()
+    for k in ALONG:
+        along(z, k).wait_recv()
+    pl.when(jnp.logical_and(is_direct, jnp.logical_not(is_home)))(along(z, 0).wait_recv)
     for m in range(MODES):
         for half in range(2):
             cols = slice(half * ROWS, (half + 1) * ROWS)
             res_out[m : m + 1, cols] = f_recv[m // 2 % NX, m // 2 // NX, m % 2, half : half + 1, :]
     res_out[...] = res_out[...] * (jnp.sqrt(2.0 * poles_in[0]) * norm)
-    for copy in a_copies + e_copies + f_copies:
+    for copy in a_copies + e_copies:
         copy.wait_send()
     @pl.when(jnp.logical_not(is_home))
     def _():
@@ -364,9 +387,19 @@
         for k, dy in cross:
             result(k, dy).wait_send()
 
-        @pl.loop(1, NZ)
+        @pl.loop(1, DIRECT)
+        def _(zz):
+            for k in range(NX):
+                along(zz, k).wait_send()
+
+        @pl.loop(DIRECT, NZ)
         def _(zz):
             summed(zz).wait_send()
+
+    @pl.when(jnp.logical_or(is_home, jnp.logical_not(is_direct)))
+    def _():
+        for k in ALONG:
+            along(z, k).wait_send()
 
 
 def scan_call(norm, q, k, v, g, poles):
@@ -401,7 +434,7 @@
             dma((5,)),
             dma((PLANE - 1,)), dma((PLANE - 1,)), dma, dma((NZ,)), dma((NZ,)), dma,
             dma((NCH, NY)), dma((NCH, NY)), dma((NZ,)), dma,
-            dma((PLANE - 1,)), dma((PLANE - 1,)), dma((NX - 1,)), dma((NX - 1,)),
+            dma((PLANE - 1,)), dma((PLANE - 1,)), dma((NZ, NX)), dma((NX,)),
         ],
         compiler_params=pltpu.CompilerParams(
             collective_id=0, has_side_effects=True, vmem_limit_bytes=54336 * 2**10

time: 39 us -> 38.5 us (0.987)
  the two profiles are of different devices: /device:TPU:32 before, /device:TPU:1 now
where the time goes in v4:
time: 38.5 us; the launch traced here: 37.8 us
  Pallas kernels  36.4 us (95%)
  other arithmetic  0.74 us (2%)
  between operations  0.64 us (2%)
    pallas_call x1, Pallas kernels, scan_call(): pl.pallas_call(functools.partial(scan_kernel, norm), out_shape=(wide, wid...  35.5 us
    pallas_call x1, Pallas kernels, finish_call(): pl.pallas_call(finish_kernel, out_shape=tuple((jax.ShapeDtypeStruct(r.sha...  0.91 us

profile of v4, /device:TPU:1, one launch (start us, length us, event | category | flops | bytes accessed | tf_op | source)
XLA Modules:
  0.0 37.8 jit_solution(11851875174021262285)
XLA Ops:
  0.6 0.7 %pad_maximum_fusion.poles_hbm = f32[2,16,256]{2,1,0:T(8,128)S(1)} fusion(f32[1,16,256]{2,1,0:T(8,128)} %bitcast.7, f32[1,16,256]{2,1,0:T(8,128)} %bitcast.8), kind=kLoop, calls=%fused_computation | loop fusion | flops 8192 | bytes 65536 | tf_op jit(solution)/shard_map/stack | solution.py:472
  1.4 35.5 %scan_states.1 = (bf16[1024,128]{1,0:T(8,128)(2,1)S(1)}, bf16[1024,128]{1,0:T(8,128)(2,1)S(1)}, bf16[1024,128]{1,0:T(8,128)(2,1)S(1)}, f32[16,256]{1,0:T(8,128)S(1)}) custom-call(bf16[1024,128]{1,0:T(8,128)(2,1)} %q_hbm.1, bf16[1024,128]{1,0:T(8,128)(2,1)} %k_hbm.1, bf16[1024,128]{1,0:T(8,128)(2,1)} %v_hbm.1, bf16[1024,128]{1,0:T(8,128)(2,1)} %g_hbm.1, ...), custom_call_target="tpu_custom_call" | custom-call | tf_op jit(solution)/shard_map/scan_states/pallas_call | solution.py:412
  36.9 0.9 %finish.1 = (bf16[1024,128]{1,0:T(8,128)(2,1)}, bf16[1024,128]{1,0:T(8,128)(2,1)}, bf16[1024,128]{1,0:T(8,128)(2,1)}, f32[16,256]{1,0:T(8,128)}) custom-call(bf16[1024,128]{1,0:T(8,128)(2,1)S(1)} %get-tuple-element.12.refs_0_, bf16[1024,128]{1,0:T(8,128)(2,1)S(1)} %get-tuple-element.13.refs_1_, bf16[1024,128]{1,0:T(8,128)(2,1)S(1)} %get-tuple-element.14.refs_2_, ...), custom_call_target="tpu_custom_call" | custom-call | tf_op jit(solution)/shard_map/finish/pallas_call | solution.py:459

commit v5 on v4

--- a/solution.py
+++ b/solution.py
@@ -23,6 +23,7 @@
 ANSWER_FIRST = (1, 2, 3, 4, 5, 6, 7, 8)
 ANSWER_LATER = (9, 15, 10, 14, 11, 13, 12)
 DIRECT = 5
+RESULT_ORDER = (1, 2, 5, 6, 7, 8, 0, 3, 4, 9, 10, 11, 12, 13, 14, 15)
 ALONG = (2, 1, 3)
 NEAR = ((0, 1), (0, 3), (1, 0))
 FAR = ((1, 2), (1, 1), (1, 3), (0, 2))
@@ -325,12 +326,13 @@
         for k, dy in cross:
             result(k, dy).wait_recv()
         r_sum[...] = (r_recv[0] + r_recv[1]) + (r_recv[2] + r_recv[3])
-        for zz in range(1, DIRECT):
-            for k in ALONG + (0,):
-                along(zz, k).start()
-        pass_on()
-        for zz in ANSWER_FIRST + ANSWER_LATER:
-            if zz >= DIRECT:
+        for zz in RESULT_ORDER:
+            if zz == HOME:
+                pass_on()
+            elif zz < DIRECT:
+                for k in ALONG + (0,):
+                    along(zz, k).start()
+            else:
                 summed(zz).start()
 
     @pl.when(jnp.logical_not(is_direct))

time: 38.5 us -> 38.1 us (0.990)
  no operation moved by 1% of the time
where the time goes in v5:
time: 38.1 us; the launch traced here: 37.8 us
  Pallas kernels  36.4 us (96%)
  other arithmetic  0.74 us (2%)
  between operations  0.64 us (2%)
    pallas_call x1, Pallas kernels, scan_call(): pl.pallas_call(functools.partial(scan_kernel, norm), out_shape=(wide, wid...  35.5 us
    pallas_call x1, Pallas kernels, finish_call(): pl.pallas_call(finish_kernel, out_shape=tuple((jax.ShapeDtypeStruct(r.sha...  0.91 us

profile of v5, /device:TPU:1, one launch (start us, length us, event | category | flops | bytes accessed | tf_op | source)
XLA Modules:
  0.0 37.8 jit_solution(10854481639505765255)
XLA Ops:
  0.6 0.7 %pad_maximum_fusion.poles_hbm = f32[2,16,256]{2,1,0:T(8,128)S(1)} fusion(f32[1,16,256]{2,1,0:T(8,128)} %bitcast.7, f32[1,16,256]{2,1,0:T(8,128)} %bitcast.8), kind=kLoop, calls=%fused_computation | loop fusion | flops 8192 | bytes 65536 | tf_op jit(solution)/shard_map/stack | solution.py:474
  1.4 35.5 %scan_states.1 = (bf16[1024,128]{1,0:T(8,128)(2,1)S(1)}, bf16[1024,128]{1,0:T(8,128)(2,1)S(1)}, bf16[1024,128]{1,0:T(8,128)(2,1)S(1)}, f32[16,256]{1,0:T(8,128)S(1)}) custom-call(bf16[1024,128]{1,0:T(8,128)(2,1)} %q_hbm.1, bf16[1024,128]{1,0:T(8,128)(2,1)} %k_hbm.1, bf16[1024,128]{1,0:T(8,128)(2,1)} %v_hbm.1, bf16[1024,128]{1,0:T(8,128)(2,1)} %g_hbm.1, ...), custom_call_target="tpu_custom_call" | custom-call | tf_op jit(solution)/shard_map/scan_states/pallas_call | solution.py:414
  36.8 0.9 %finish.1 = (bf16[1024,128]{1,0:T(8,128)(2,1)}, bf16[1024,128]{1,0:T(8,128)(2,1)}, bf16[1024,128]{1,0:T(8,128)(2,1)}, f32[16,256]{1,0:T(8,128)}) custom-call(bf16[1024,128]{1,0:T(8,128)(2,1)S(1)} %get-tuple-element.12.refs_0_, bf16[1024,128]{1,0:T(8,128)(2,1)S(1)} %get-tuple-element.13.refs_1_, bf16[1024,128]{1,0:T(8,128)(2,1)S(1)} %get-tuple-element.14.refs_2_, ...), custom_call_target="tpu_custom_call" | custom-call | tf_op jit(solution)/shard_map/finish/pallas_call | solution.py:461

commit v6 on v5

--- a/solution.py
+++ b/solution.py
@@ -406,7 +406,7 @@
 
 def scan_call(norm, q, k, v, g, poles):
     hbm = pl.BlockSpec(memory_space=pltpu.HBM)
-    big = pltpu.VMEM((CHN, ROWS), F32)
+    big = pltpu.VMEM((CHN + SUB, ROWS), F32)
     half = pltpu.VMEM((CHN, ROWS), jnp.bfloat16)
     table = pltpu.VMEM((MODES, SUB, ROWS), F32)
     dma = pltpu.SemaphoreType.DMA

time: 38.1 us -> 38.1 us (level)
  no operation moved by 1% of the time
where the time goes in v6:
time: 38.1 us; the launch traced here: 37.8 us
  Pallas kernels  36.4 us (96%)
  other arithmetic  0.74 us (2%)
  between operations  0.64 us (2%)
    pallas_call x1, Pallas kernels, scan_call(): pl.pallas_call(functools.partial(scan_kernel, norm), out_shape=(wide, wid...  35.5 us
    pallas_call x1, Pallas kernels, finish_call(): pl.pallas_call(finish_kernel, out_shape=tuple((jax.ShapeDtypeStruct(r.sha...  0.91 us

profile of v6, /device:TPU:1, one launch (start us, length us, event | category | flops | bytes accessed | tf_op | source)
XLA Modules:
  0.0 37.8 jit_solution(5381584964258359125)
XLA Ops:
  0.6 0.7 %pad_maximum_fusion.poles_hbm = f32[2,16,256]{2,1,0:T(8,128)S(1)} fusion(f32[1,16,256]{2,1,0:T(8,128)} %bitcast.7, f32[1,16,256]{2,1,0:T(8,128)} %bitcast.8), kind=kLoop, calls=%fused_computation | loop fusion | flops 8192 | bytes 65536 | tf_op jit(solution)/shard_map/stack | solution.py:474
  1.4 35.5 %scan_states.1 = (bf16[1024,128]{1,0:T(8,128)(2,1)S(1)}, bf16[1024,128]{1,0:T(8,128)(2,1)S(1)}, bf16[1024,128]{1,0:T(8,128)(2,1)S(1)}, f32[16,256]{1,0:T(8,128)S(1)}) custom-call(bf16[1024,128]{1,0:T(8,128)(2,1)} %q_hbm.1, bf16[1024,128]{1,0:T(8,128)(2,1)} %k_hbm.1, bf16[1024,128]{1,0:T(8,128)(2,1)} %v_hbm.1, bf16[1024,128]{1,0:T(8,128)(2,1)} %g_hbm.1, ...), custom_call_target="tpu_custom_call" | custom-call | tf_op jit(solution)/shard_map/scan_states/pallas_call | solution.py:414
  36.8 0.9 %finish.1 = (bf16[1024,128]{1,0:T(8,128)(2,1)}, bf16[1024,128]{1,0:T(8,128)(2,1)}, bf16[1024,128]{1,0:T(8,128)(2,1)}, f32[16,256]{1,0:T(8,128)}) custom-call(bf16[1024,128]{1,0:T(8,128)(2,1)S(1)} %get-tuple-element.12.refs_0_, bf16[1024,128]{1,0:T(8,128)(2,1)S(1)} %get-tuple-element.13.refs_1_, bf16[1024,128]{1,0:T(8,128)(2,1)S(1)} %get-tuple-element.14.refs_2_, ...), custom_call_target="tpu_custom_call" | custom-call | tf_op jit(solution)/shard_map/finish/pallas_call | solution.py:461

commit v7 on v6

--- a/solution.py
+++ b/solution.py
@@ -73,7 +73,7 @@
     def cross_id(k, dy):
         return (y_plus[dy] * NZ + HOME) * NX + x, ch_plus[k]
 
-    cross = [(k, dy) for k in range(NCH) for dy in reversed(range(NY)) if k or dy]
+    cross = [(k, dy) for k in (2, 1, 3, 0) for dy in reversed(range(NY)) if k or dy]
 
     loads = [
         pltpu.make_async_copy(src, dst, in_sem.at[i])

time: 38.1 us -> 38.1 us (level)
  no operation moved by 1% of the time
where the time goes in v7:
time: 38.1 us; the launch traced here: 37.7 us
  Pallas kernels  36.4 us (96%)
  other arithmetic  0.74 us (2%)
  between operations  0.64 us (2%)
    pallas_call x1, Pallas kernels, scan_call(): pl.pallas_call(functools.partial(scan_kernel, norm), out_shape=(wide, wid...  35.4 us
    pallas_call x1, Pallas kernels, finish_call(): pl.pallas_call(finish_kernel, out_shape=tuple((jax.ShapeDtypeStruct(r.sha...  0.91 us

profile of v7, /device:TPU:1, one launch (start us, length us, event | category | flops | bytes accessed | tf_op | source)
XLA Modules:
  0.0 37.7 jit_solution(14121534938012781574)
XLA Ops:
  0.6 0.7 %pad_maximum_fusion.poles_hbm = f32[2,16,256]{2,1,0:T(8,128)S(1)} fusion(f32[1,16,256]{2,1,0:T(8,128)} %bitcast.7, f32[1,16,256]{2,1,0:T(8,128)} %bitcast.8), kind=kLoop, calls=%fused_computation | loop fusion | flops 8192 | bytes 65536 | tf_op jit(solution)/shard_map/stack | solution.py:474
  1.4 35.4 %scan_states.1 = (bf16[1024,128]{1,0:T(8,128)(2,1)S(1)}, bf16[1024,128]{1,0:T(8,128)(2,1)S(1)}, bf16[1024,128]{1,0:T(8,128)(2,1)S(1)}, f32[16,256]{1,0:T(8,128)S(1)}) custom-call(bf16[1024,128]{1,0:T(8,128)(2,1)} %q_hbm.1, bf16[1024,128]{1,0:T(8,128)(2,1)} %k_hbm.1, bf16[1024,128]{1,0:T(8,128)(2,1)} %v_hbm.1, bf16[1024,128]{1,0:T(8,128)(2,1)} %g_hbm.1, ...), custom_call_target="tpu_custom_call" | custom-call | tf_op jit(solution)/shard_map/scan_states/pallas_call | solution.py:414
  36.8 0.9 %finish.1 = (bf16[1024,128]{1,0:T(8,128)(2,1)}, bf16[1024,128]{1,0:T(8,128)(2,1)}, bf16[1024,128]{1,0:T(8,128)(2,1)}, f32[16,256]{1,0:T(8,128)}) custom-call(bf16[1024,128]{1,0:T(8,128)(2,1)S(1)} %get-tuple-element.12.refs_0_, bf16[1024,128]{1,0:T(8,128)(2,1)S(1)} %get-tuple-element.13.refs_1_, bf16[1024,128]{1,0:T(8,128)(2,1)S(1)} %get-tuple-element.14.refs_2_, ...), custom_call_target="tpu_custom_call" | custom-call | tf_op jit(solution)/shard_map/finish/pallas_call | solution.py:461
